TPU v7x, 32 devices: a whole 2x2x4 slice. The times are simulated.
32 devices in a mesh: pair: 2 (over x), dp: 16 (over z, y, core).
Axes of the slice: x: 2, y: 2, z: 4, core: 2. Of those that a mesh axis runs over, the one named last changes fastest.
Arguments:
- states: bfloat16 [2, 18944, 512], P('pair', 'dp'), may hold values from -6 to 6
- norm_gains: bfloat16 [2, 512, 2], P('pair'), may hold values from 0.5 to 1.5
- w_qkv: bfloat16 [2, 512, 1536], P('pair'), may hold values from -0.25 to 0.25
- w_out: bfloat16 [2, 512, 512], P('pair'), may hold values from -2 to 2
- w_up: bfloat16 [2, 512, 2048], P('pair'), may hold values from -0.25 to 0.25
- w_down: bfloat16 [2, 2048, 512], P('pair'), may hold values from -0.125 to 0.125
- w_head: bfloat16 [2, 512, 256], P('pair'), may hold values from -0.25 to 0.25
- task_ids: int32 [64], P('dp'), may hold values from 0 to 31
- chosen: int32 [18944], P('dp'), may hold values from 0 to 255
- reward: int32 [18944], P('dp'), may hold values 0 or 1
- finished: int32 [18944], P('dp'), may hold values 0 or 1
Outputs:
- q_values: bfloat16 [18944, 256], P('dp', 'pair')
- grad_states: bfloat16 [18944, 512], P('dp', 'pair')
- grad_gains: float32 [512, 2], P('dp', 'pair')
- grad_qkv: float32 [512, 1536], P('dp', 'pair')
- grad_out: float32 [512, 512], P('dp', 'pair')
- grad_up: float32 [512, 2048], P('dp', 'pair')
- grad_down: float32 [2048, 512], P('dp', 'pair')
- grad_head: float32 [512, 256], P('dp', 'pair')
- new_gains: float32 [512, 2], P('dp', 'pair')
- new_qkv: float32 [512, 1536], P('dp', 'pair')
- new_out: float32 [512, 512], P('dp', 'pair')
- new_up: float32 [512, 2048], P('dp', 'pair')
- new_down: float32 [2048, 512], P('dp', 'pair')
- new_head: float32 [512, 256], P('dp', 'pair')
- stats: float32 [5], replicated
All inputs are finite; a program needn't handle non-finite values. No bound on the sum of `reward` or of `finished` on one device may be relied on, other than what follows from the above.
Results may differ from a plain program's by a relative error of at most 0.012.
Values may be sent and summed in bfloat16 or wider, within the bound.
A program may use at most 192 MiB of HBM per device.

v0:
```python
import jax
import jax.numpy as jnp
from jax import lax
from jax.sharding import PartitionSpec as P

HEAD_DIM = 64
L = 296
TASKS = 32


EPSILON = 1e-06
DISCOUNT = 0.98
SOFT_RATE = 0.2
SCORE_SCALE = 0.125
NEG_LARGE = -1000000000.0
LOWEST = -1e30


def from_behind(value, axis, by):
    count = lax.axis_size(axis)
    pairs = [(i, i + by) for i in range(count) if 0 <= i + by < count]
    return lax.ppermute(value, axis, pairs)


def swapped(value, axis, bit):
    return lax.ppermute(value, axis, [(i, i ^ 1 << bit) for i in range(lax.axis_size(axis))])


def combined_all(part, axis, combine):
    gathered = jax.tree.map(lambda a: lax.all_gather(a, axis), part)

    def take(source):
        return jax.tree.map(lambda a: lax.dynamic_index_in_dim(a, source, 0, False), gathered)

    return lax.fori_loop(
        1, lax.axis_size(axis), lambda source, state: combine(state, take(source)), take(0)
    )


def normalize(values, gain_row):
    return (
        values * lax.rsqrt(jnp.mean(values * values, axis=-1, keepdims=True) + EPSILON) * gain_row
    )


def inner_rows(left, right):
    return lax.dot_general(
        left, right, (((0,), (0,)), ((), ())), preferred_element_type=jnp.float32
    )


def times_back(left, right):
    return lax.dot_general(
        left, right, (((1,), (1,)), ((), ())), preferred_element_type=jnp.float32
    )


def split_heads(qkv_rows, seq_count):
    heads_here = qkv_rows.shape[1] // (3 * HEAD_DIM)
    shaped = qkv_rows.reshape(seq_count, L, 3, heads_here, HEAD_DIM)
    return (shaped[:, :, 0], shaped[:, :, 1], shaped[:, :, 2])


def masked_scores(queries, key_rows):
    raw = (
        jnp.einsum("sqhd,skhd->shqk", queries, key_rows, preferred_element_type=jnp.float32)
        * SCORE_SCALE
    )
    causal = lax.broadcasted_iota(jnp.int32, (L, L), 0) >= lax.broadcasted_iota(
        jnp.int32, (L, L), 1
    )
    return jnp.where(causal, raw, NEG_LARGE)


def attend(queries, key_rows, value_rows):
    scores = masked_scores(queries, key_rows)
    largest = jnp.max(scores, axis=-1, keepdims=True)
    raised = jnp.exp(scores - largest)
    totals = jnp.sum(raised, axis=-1, keepdims=True)
    probs = (raised / totals).astype(jnp.bfloat16)
    mixed = jnp.einsum("shqk,skhd->sqhd", probs, value_rows, preferred_element_type=jnp.float32)
    return (mixed, largest + jnp.log(totals))


def attend_back(queries, key_rows, value_rows, log_totals, grad_mixed):
    probs = jnp.exp(masked_scores(queries, key_rows) - log_totals)
    grad_values = jnp.einsum(
        "shqk,sqhd->skhd",
        probs.astype(jnp.bfloat16),
        grad_mixed,
        preferred_element_type=jnp.float32,
    )
    grad_probs = jnp.einsum(
        "sqhd,skhd->shqk", grad_mixed, value_rows, preferred_element_type=jnp.float32
    )
    centred = grad_probs - jnp.sum(probs * grad_probs, axis=-1, keepdims=True)
    grad_scores = (probs * centred).astype(jnp.bfloat16)
    grad_queries = (
        jnp.einsum("shqk,skhd->sqhd", grad_scores, key_rows, preferred_element_type=jnp.float32)
        * SCORE_SCALE
    )
    grad_keys = (
        jnp.einsum("shqk,sqhd->skhd", grad_scores, queries, preferred_element_type=jnp.float32)
        * SCORE_SCALE
    )
    return jnp.stack([grad_queries, grad_keys, grad_values], axis=2)


def forward(tokens, params):
    gain_pair, w_qkv, w_out, w_up, w_down, w_head = params
    seq_count = tokens.shape[0] // L
    normed_one = normalize(tokens, gain_pair[:, 0].astype(jnp.float32)).astype(jnp.bfloat16)
    qkv_rows = jnp.dot(normed_one, w_qkv, preferred_element_type=jnp.float32).astype(jnp.bfloat16)
    queries, key_rows, value_rows = split_heads(qkv_rows, seq_count)
    mixed, log_totals = attend(queries, key_rows, value_rows)
    attended = mixed.reshape(tokens.shape[0], -1).astype(jnp.bfloat16)
    middle = tokens + jnp.dot(attended, w_out, preferred_element_type=jnp.float32)
    normed_two = normalize(middle, gain_pair[:, 1].astype(jnp.float32)).astype(jnp.bfloat16)
    upper = jnp.dot(normed_two, w_up, preferred_element_type=jnp.float32)
    active = jax.nn.gelu(upper).astype(jnp.bfloat16)
    final_rows = middle + jnp.dot(active, w_down, preferred_element_type=jnp.float32)
    final_low = final_rows.astype(jnp.bfloat16)
    qvals = jnp.dot(final_low, w_head, preferred_element_type=jnp.float32)
    stored = (
        normed_one,
        queries,
        key_rows,
        value_rows,
        log_totals,
        attended,
        middle,
        normed_two,
        upper,
        active,
        final_low,
    )
    return (qvals, stored)


def backward(tokens, params, stored, grad_q):
    gain_pair, w_qkv, w_out, w_up, w_down, w_head = params
    (
        normed_one,
        queries,
        key_rows,
        value_rows,
        log_totals,
        attended,
        middle,
        normed_two,
        upper,
        active,
        final_low,
    ) = stored
    gain_one = gain_pair[:, 0].astype(jnp.float32)
    gain_two = gain_pair[:, 1].astype(jnp.float32)
    grad_qlow = grad_q.astype(jnp.bfloat16)
    grad_head = inner_rows(final_low, grad_qlow)
    grad_final = times_back(grad_qlow, w_head)
    grad_ffn = grad_final.astype(jnp.bfloat16)
    grad_down = inner_rows(active, grad_ffn)
    grad_active = times_back(grad_ffn, w_down)
    gelu_value, gelu_back = jax.vjp(jax.nn.gelu, upper)
    grad_upper = gelu_back(grad_active)[0].astype(jnp.bfloat16)
    grad_up = inner_rows(normed_two, grad_upper)
    grad_two = times_back(grad_upper, w_up)
    norm_value, norm_back = jax.vjp(normalize, middle, gain_two)
    grad_inside, grad_gain_two = norm_back(grad_two)
    grad_middle = grad_final + grad_inside
    grad_branch = grad_middle.astype(jnp.bfloat16)
    grad_out = inner_rows(attended, grad_branch)
    grad_mixed = times_back(grad_branch, w_out).astype(jnp.bfloat16).reshape(queries.shape)
    grad_rows = attend_back(queries, key_rows, value_rows, log_totals, grad_mixed)
    grad_rows = grad_rows.reshape(tokens.shape[0], -1).astype(jnp.bfloat16)
    grad_qkv = inner_rows(normed_one, grad_rows)
    grad_one = times_back(grad_rows, w_qkv)
    first_value, first_back = jax.vjp(normalize, tokens, gain_one)
    grad_inner, grad_gain_one = first_back(grad_one)
    grad_tokens = grad_middle + grad_inner
    grad_gains = jnp.stack([grad_gain_one, grad_gain_two], axis=1)
    return (grad_tokens, (grad_gains, grad_qkv, grad_out, grad_up, grad_down, grad_head))


def cols_half(matrix, half):
    width = matrix.shape[1] // 2
    return lax.dynamic_slice_in_dim(matrix, half * width, width, 1)


def owned_piece(matrix, block, half, blocks):
    height = matrix.shape[0] // blocks
    return cols_half(lax.dynamic_slice_in_dim(matrix, block * height, height, 0), half).astype(
        jnp.float32
    )


def combine_stats(first_part, second_part):
    return (first_part[0] + second_part[0], jnp.maximum(first_part[1], second_part[1]))


def td_loss(qvals, aims, row_weight, chosen):
    picked_mask = chosen[:, None] == jnp.arange(qvals.shape[1], dtype=jnp.int32)[None, :]
    picked = jnp.sum(jnp.where(picked_mask, qvals, 0.0), axis=1)
    differ = picked - aims
    loss_local = jnp.sum(row_weight * 0.5 * differ * differ)
    grad_q = jnp.where(picked_mask, (row_weight * differ)[:, None], 0.0)
    return (loss_local, grad_q)


def local(
    states, norm_gains, w_qkv, w_out, w_up, w_down, w_head, task_ids, chosen, reward, finished
):
    pair_index = lax.axis_index("pair")
    data_index = lax.axis_index("dp")
    data_count = lax.axis_size("dp")
    online = pair_index == 0
    other = 1 - pair_index
    params = (norm_gains[0], w_qkv[0], w_out[0], w_up[0], w_down[0], w_head[0])
    row_count = states.shape[1]
    seq_count = row_count // L
    table = (task_ids[:, None] == jnp.arange(TASKS, dtype=jnp.int32)[None, :]).astype(jnp.float32)
    counts = lax.psum(jnp.sum(table, axis=0), "dp")
    seq_weight = seq_count * data_count / (TASKS * jnp.sum(table * counts[None, :], axis=1))
    row_weight = jnp.broadcast_to(seq_weight[:, None], (seq_count, L)).reshape(row_count)
    tokens = states[0].astype(jnp.float32)
    qvals, stored = forward(tokens, params)
    row_top = jnp.max(qvals, axis=1)
    bootstrap = (
        reward.astype(jnp.float32) + DISCOUNT * (1.0 - finished.astype(jnp.float32)) * row_top
    )
    aims = from_behind(bootstrap, "pair", -1)
    loss_local, grad_q = td_loss(qvals, aims, row_weight, chosen)

    def run_back():
        return backward(tokens, params, stored, grad_q)

    def skip_back():
        return (
            jnp.zeros_like(tokens),
            tuple((jnp.zeros(weight.shape, jnp.float32) for weight in params)),
        )

    grad_tokens, grads = lax.cond(online, run_back, skip_back)
    q_low = qvals.astype(jnp.bfloat16)
    grad_low = grad_tokens.astype(jnp.bfloat16)
    got_q, got_grad = from_behind((cols_half(q_low, 1), cols_half(grad_low, 1)), "pair", 1)
    q_values = jnp.where(online, cols_half(q_low, 0), got_q)
    grad_states = jnp.where(online, cols_half(grad_low, 0), got_grad)
    total_top = jnp.sum(row_top)
    best_top = jnp.max(row_top)
    partial_sums = jnp.stack(
        [
            jnp.where(online, loss_local, 0.0),
            jnp.where(online, total_top, 0.0),
            jnp.where(online, 0.0, total_top),
        ]
    )
    partial_tops = jnp.stack(
        [jnp.where(online, best_top, LOWEST), jnp.where(online, LOWEST, best_top)]
    )
    own_pieces = tuple(
        (owned_piece(weight, data_index, pair_index, data_count) for weight in params)
    )
    sent_pieces = tuple((owned_piece(weight, data_index, other, data_count) for weight in params))
    reduced = (
        lax.psum_scatter(grads[0], "dp", scatter_dimension=0, tiled=True),
        lax.psum_scatter(grads[1], "dp", scatter_dimension=0, tiled=True),
        lax.psum_scatter(grads[2], "dp", scatter_dimension=0, tiled=True),
        lax.psum_scatter(grads[3], "dp", scatter_dimension=0, tiled=True),
        lax.psum_scatter(grads[4], "dp", scatter_dimension=0, tiled=True),
        lax.psum_scatter(grads[5], "dp", scatter_dimension=0, tiled=True),
    )
    outgoing = tuple((cols_half(reduced_part, other) for reduced_part in reduced)) + sent_pieces
    incoming = swapped(
        (
            outgoing[0],
            outgoing[1],
            outgoing[2],
            outgoing[3],
            outgoing[4],
            outgoing[5],
            outgoing[6],
            outgoing[7],
            outgoing[8],
            outgoing[9],
            outgoing[10],
            outgoing[11],
        ),
        "pair",
        0,
    )
    grad_pieces = tuple(
        (
            cols_half(reduced_part, pair_index) + incoming[position]
            for position, reduced_part in enumerate(reduced)
        )
    )
    new_pieces = []
    for position in range(6):
        own_piece = own_pieces[position]
        theirs = incoming[6 + position]
        online_part = jnp.where(online, own_piece, theirs)
        target_part = jnp.where(online, theirs, own_piece)
        new_pieces.append(target_part + SOFT_RATE * (online_part - target_part))
    all_sums, all_tops = combined_all((partial_sums, partial_tops), ("pair", "dp"), combine_stats)
    token_total = row_count * data_count
    stats = jnp.stack(
        [
            all_sums[0] / token_total,
            all_sums[1] / token_total,
            all_tops[0],
            all_sums[2] / token_total,
            all_tops[1],
        ]
    )
    return (
        q_values,
        grad_states,
        grad_pieces[0],
        grad_pieces[1],
        grad_pieces[2],
        grad_pieces[3],
        grad_pieces[4],
        grad_pieces[5],
        new_pieces[0],
        new_pieces[1],
        new_pieces[2],
        new_pieces[3],
        new_pieces[4],
        new_pieces[5],
        stats,
    )


def solution(mesh):
    placed = (
        P("pair", "dp", None),
        P("pair", None, None),
        P("pair", None, None),
        P("pair", None, None),
        P("pair", None, None),
        P("pair", None, None),
        P("pair", None, None),
        P("dp"),
        P("dp"),
        P("dp"),
        P("dp"),
    )
    return jax.shard_map(
        local,
        mesh=mesh,
        in_specs=placed,
        out_specs=(
            P("dp", "pair"),
            P("dp", "pair"),
            P("dp", "pair"),
            P("dp", "pair"),
            P("dp", "pair"),
            P("dp", "pair"),
            P("dp", "pair"),
            P("dp", "pair"),
            P("dp", "pair"),
            P("dp", "pair"),
            P("dp", "pair"),
            P("dp", "pair"),
            P("dp", "pair"),
            P("dp", "pair"),
            P(),
        ),
        check_vma=False,
    )
```

profile of v0, /device:TPU:0, one launch (start us, length us, event | category | flops | bytes accessed | tf_op | source)
XLA Modules:
  0.0 669.4 jit_solution(6608478708013555947)
XLA Ops:
  9.6 5.8 convolution_convert_fusion.1
  15.4 9.8 %reshape.272 = bf16[4,296,3,8,64]{4,3,2,1,0:T(8,128)(2,1)} reshape(bf16[1184,1536]{1,0:T(8,128)(2,1)} %convolution_convert_fusion.1) | data formatting | bytes 7274496 | tf_op jit(solution)/shard_map/reshape | solution.py:60
  25.2 6.2 fusion.82
  38.1 4.2 copy.109
  42.2 7.2 %fusion.26 = (f32[4,8,296]{2,1,0:T(8,128)S(1)}, f32[4,8,296,296]{2,3,1,0:T(8,128)}) fusion(pred[296,296]{0,1:T(8,128)(4,1)S(1)} %iota_compare_fusion.2, bf16[4,296,1,8,64]{1,4,3,0,2:T(8,128)(2,1)S(1)} %copy.111, bf16[4,296,1,8,64]{1,4,3,0,2:T(8,128)(2,1)S(1)} %copy.110), kind=kOutput, calls=%fused_computation.60 | convolution fusion | flops 367276800 | bytes 13765184 | tf_op jit(solution)/shard_map/sqhd,skhd->shqk/dot_general | solution.py:66
  49.5 8.5 %fusion.27 = f32[4,8,296]{2,1,0:T(8,128)S(1)} fusion(f32[4,8,296,296]{2,3,1,0:T(8,128)} %get-tuple-element.379, f32[4,8,296]{2,1,0:T(8,128)S(1)} %get-tuple-element.378, pred[296,296]{0,1:T(8,128)(4,1)S(1)} %iota_compare_fusion.2), kind=kLoop, calls=%fused_computation.61 | loop fusion | flops 11205376 | bytes 11378240 | tf_op jit(solution)/shard_map/reduce_sum | solution.py:79
  58.0 9.5 %fusion.40 = bf16[4,296,8,64]{1,3,2,0:T(8,128)(2,1)S(1)} fusion(f32[4,8,296,296]{2,3,1,0:T(8,128)} %get-tuple-element.379, f32[4,8,296]{2,1,0:T(8,128)S(1)} %fusion.27, f32[4,8,296]{2,1,0:T(8,128)S(1)} %get-tuple-element.378, pred[296,296]{0,1:T(8,128)(4,1)S(1)} %iota_compare_fusion.2, bf16[4,296,1,8,64]{1,4,3,0,2:T(8,128)(2,1)S(1)} %copy-done.15), kind=kOutput, calls=%fused_computation.83 | convolution fusion | flops 372893696 | bytes 13803072 | tf_op jit(solution)/shard_map/shqk,skhd->sqhd/dot_general | solution.py:81
  71.2 3.9 convert_element_type.225
  80.3 6.7 %fusion.35 = (bf16[1184,2048]{1,0:T(8,128)(2,1)S(1)}, f32[1184,2048]{1,0:T(8,128)}) fusion(bf16[1184,512]{1,0:T(8,128)(2,1)S(1)} %multiply_convert_fusion.4, bf16[1,512,2048]{2,1,0:T(8,128)(2,1)S(1)} %copy-done.40), kind=kOutput, calls=%fused_computation.69 | convolution fusion | flops 2504851456 | bytes 17858560 | tf_op jit(solution)/shard_map/dot_general | solution.py:119
  97.8 34.9 %psum.7 = f32[32]{0:T(128)S(1)} all-reduce(f32[32]{0:T(128)S(1)} %convert_reduce_fusion), channel_id=1, replica_groups=mesh['pair'=2,'dp'=16] {'dp'}, use_global_device_ids=true, to_apply=%region_5.6 | all-reduce | flops 32 | bytes 256 | tf_op jit(solution)/shard_map/psum | solution.py:221
  136.4 126.6 %conditional.1 = (bf16[1184,512]{1,0:T(8,128)(2,1)}, f32[512,2]{0,1:T(2,128)}, f32[512,1536]{0,1:T(8,128)}, f32[512,512]{0,1:T(8,128)}, f32[512,2048]{0,1:T(8,12...) conditional(s32[]{:T(128)} %convert_element_type.232, () %tuple.38, (f32[1184]{0:T(1024)S(1)}, f32[1184]{0:T(1024)S(1)}, ...), branch_computations={%region_9.10_spmd, %region_10.18_spmd} | conditional | flops 17415020544 | bytes 441093088 | solution.py:242
  141.2 10.2 %fusion.6 = bf16[1184,2048]{1,0:T(8,128)(2,1)S(1)} fusion(f32[1184,2048]{1,0:T(8,128)} %get-tuple-element.186, bf16[2048,512]{1,0:T(8,128)(2,1)S(1)} %copy-done.39, f32[1184,512]{1,0:T(8,128)S(1)} %fusion.25), kind=kOutput, calls=%fused_computation.11 | convolution fusion | flops 2532130816 | bytes 19070976 | tf_op jit(solution)/shard_map/cond/branch_1_fun/dot_general | solution.py:53
  165.9 4.6 fusion.86
  171.2 13.0 %multiply_reduce_fusion = (f32[4,8,296]{2,1,0:T(8,128)}, f32[4,8,296,296]{2,3,1,0:T(8,128)}) fusion(f32[4,8,296,296]{2,3,1,0:T(8,128)S(1)} %fusion.86, f32[4,8,296]{2,1,0:T(8,128)} %log_add_fusion, bf16[4,296,8,64]{1,3,2,0:T(8,128)(2,1)} %copy-done.5, bf16[4,296,8,64]{1,3,2,0:T(8,128)(2,1)} %copy-done.3, pred[296,296]{0,1:T(8,128)(4,1)S(1)} %iota_compare_fusion), kind=kOutput, calls=%fused_computation.1 | convolution fusion | flops 372884224 | bytes 25017920 | tf_op jit(solution)/shard_map/cond/branch_1_fun/sqhd,skhd->shqk/dot_general | solution.py:66
  184.2 9.4 %fusion.14 = bf16[4,296,1,8,64]{1,4,3,0,2:T(8,128)(2,1)} fusion(bf16[4,296,8,64]{1,3,2,0:T(8,128)(2,1)} %copy.81, f32[4,8,296,296]{2,3,1,0:T(8,128)} %get-tuple-element.359), kind=kOutput, calls=%fused_computation.32 | convolution fusion | flops 362285056 | bytes 13639680 | tf_op jit(solution)/shard_map/cond/branch_1_fun/shqk,sqhd->skhd/dot_general | solution.py:87
  193.6 9.1 %multiply_convert_fusion = bf16[4,8,296,296]{2,3,1,0:T(8,128)(2,1)} fusion(f32[4,8,296,296]{2,3,1,0:T(8,128)} %get-tuple-element.359, f32[4,8,296,296]{2,3,1,0:T(8,128)S(1)} %fusion.86, f32[4,8,296]{2,1,0:T(8,128)S(1)} %copy-done.29), kind=kLoop, calls=%fused_computation | loop fusion | flops 8411136 | bytes 28075008 | tf_op jit(solution)/shard_map/cond/branch_1_fun/convert_element_type | solution.py:97
  202.7 5.8 fusion.18
  211.2 6.3 copy.86
  217.5 8.3 %convert_element_type.163 = bf16[1184,1536]{0,1:T(8,128)(2,1)} reshape(bf16[4,296,3,8,64]{1,0,4,3,2:T(4,128)(2,1)} %copy.86) | data formatting | bytes 7274496 | tf_op jit(solution)/shard_map/cond/branch_1_fun/convert_element_type | solution.py:174
  225.9 6.4 multiply_reduce_fusion.2
  241.5 3.9 convert_element_type.167
  248.7 7.8 %convolution_bitcast_fusion.1 = f32[512,2048]{0,1:T(8,128)} fusion(bf16[1184,2048]{1,0:T(8,128)(2,1)} %copy-done.51, bf16[1184,512]{1,0:T(8,128)(2,1)} %get-tuple-element.200), kind=kOutput, calls=%fused_computation.18 | convolution fusion | flops 2483027968 | bytes 10256384 | tf_op jit(solution)/shard_map/cond/branch_1_fun/dot_general | solution.py:47
  256.6 4.5 convolution_bitcast_fusion
  273.1 5.4 copy.96
  293.2 5.5 copy.97
  299.5 36.9 %all-reduce.2 = (f32[96]{0:T(128)S(1)}, f32[64]{0:T(128)S(1)}) all-reduce(f32[96]{0:T(128)S(1)} %maximum_dynamic-update-slice_fusion, f32[64]{0:T(128)S(1)} %maximum_dynamic-update-slice_fusion.1), channel_id=2, replica_groups=mesh['pair'=2,'dp'=16] {'pair','dp'}, use_global_device_ids=true, to_apply=%add | all-reduce | flops 160 | bytes 1280
  352.7 3.9 collective-permute-start.2
  369.6 4.7 reduce-scatter.17.cloned.1.call-done
  376.5 58.3 %reduce-scatter.11.cloned.1.call-done = f32[32,512]{1,0:T(8,128)} async-done(((f32[512,512]{1,0:T(8,128)}), f32[32,512]{1,0:T(8,128)}) %reduce-scatter.11.cloned.1.call-update) | async-done | bytes 65552 | tf_op jit(solution)/shard_map/reduce_scatter | solution.py:267
  440.9 62.9 %reduce-scatter.9.cloned.1.call-done = f32[32,1536]{1,0:T(8,128)} async-done(((f32[512,1536]{1,0:T(8,128)}), f32[32,1536]{1,0:T(8,128)}) %reduce-scatter.9.cloned.1.call-update) | async-done | bytes 196624 | tf_op jit(solution)/shard_map/reduce_scatter | solution.py:266
  506.1 72.9 %reduce-scatter.13.cloned.1.call-done = f32[32,2048]{1,0:T(8,128)} async-done(((f32[512,2048]{1,0:T(8,128)}), f32[32,2048]{1,0:T(8,128)}) %reduce-scatter.13.cloned.1.call-update) | async-done | bytes 262160 | tf_op jit(solution)/shard_map/reduce_scatter | solution.py:268
  583.1 71.7 %reduce-scatter.15.cloned.1.call-done = f32[128,512]{1,0:T(8,128)} async-done(((f32[2048,512]{1,0:T(8,128)}), f32[128,512]{1,0:T(8,128)}) %reduce-scatter.15.cloned.1.call-update) | async-done | bytes 262160 | tf_op jit(solution)/shard_map/reduce_scatter | solution.py:269
  (302 shorter events, 141.5 us)
Async XLA Ops:
  7.2 336.8 %reduce-scatter.19.cloned.1.call-start = ((), (), s32[]{:S(2)}) async-start(), calls=%async_computation.11 | async-start | bytes 278528
  49.5 8.6 %copy-start.15 = (bf16[4,296,1,8,64]{1,4,3,0,2:T(8,128)(2,1)S(1)}, bf16[4,296,1,8,64]{1,4,3,0,2:T(8,128)(2,1)}, u32[]{:S(2)}) copy-start(bf16[4,296,1,8,64]{1,4,3,0,2:T(8,128)(2,1)} %copy.109) | copy-start | bytes 3637252
  77.8 9.2 %copy-start.11 = (f32[1184,512]{1,0:T(8,128)}, f32[1184,512]{1,0:T(8,128)S(1)}, u32[]{:S(2)}) copy-start(f32[1184,512]{1,0:T(8,128)S(1)} %get-tuple-element.381) | copy-start | bytes 7274500
  93.1 41.9 %collective-permute-start.1 = (f32[1184]{0:T(1024)}, f32[1184]{0:T(1024)}, u32[]{:S(2)}, u32[]{:S(2)}) collective-permute-start(f32[1184]{0:T(1024)} %get-tuple-element.370), channel_id=1, source_target_pairs={{16,0},{17,1},{18,2},{19,3},{20,4},{21,5},{22,6},{23,7},{24,8},{25... | collective-permute-start | bytes 14216 | tf_op jit(solution)/shard_map/ppermute | solution.py:22
  138.4 16.8 %copy-start.7 = (f32[1184,512]{1,0:T(8,128)}, f32[1184,512]{1,0:T(8,128)S(1)}, u32[]{:S(2)}) copy-start(f32[1184,512]{1,0:T(8,128)S(1)} %fusion.25) | copy-start | bytes 7274500 | tf_op jit(solution)/shard_map/cond
  141.2 10.2 %copy-start.41 = (bf16[512,2048]{1,0:T(8,128)(2,1)S(1)}, bf16[512,2048]{1,0:T(8,128)(2,1)}, u32[]{:S(2)}) copy-start(bf16[512,2048]{1,0:T(8,128)(2,1)} %get-tuple-element.187) | copy-start | bytes 6291460 | tf_op jit(solution)/shard_map/cond
  184.2 9.4 %copy-start.29 = (f32[4,8,296]{2,1,0:T(8,128)S(1)}, f32[4,8,296]{2,1,0:T(8,128)}, u32[]{:S(2)}) copy-start(f32[4,8,296]{2,1,0:T(8,128)} %get-tuple-element.358) | copy-start | bytes 113668 | tf_op jit(solution)/shard_map/cond
  193.6 9.1 %copy-start.6 = (bf16[4,296,8,64]{1,3,2,0:T(8,128)(2,1)S(1)}, bf16[4,296,8,64]{1,3,2,0:T(8,128)(2,1)}, u32[]{:S(2)}) copy-start(bf16[4,296,8,64]{1,3,2,0:T(8,128)(2,1)} %copy-done.5) | copy-start | bytes 3637252 | tf_op jit(solution)/shard_map/cond
  217.5 8.3 %copy-start.34 = (f32[1184]{0:T(1024)S(1)}, f32[1184]{0:T(1024)}, u32[]{:S(2)}) copy-start(f32[1184]{0:T(1024)} %fusion.24) | copy-start | bytes 14212 | tf_op jit(solution)/shard_map/cond
  217.5 8.4 %copy-start.37 = (f32[512,1]{0,1:T(1,128)S(1)}, f32[512,1]{0,1:T(1,128)}, u32[]{:S(2)}) copy-start(f32[512,1]{0,1:T(1,128)} %get-tuple-element.355) | copy-start | bytes 6148 | tf_op jit(solution)/shard_map/cond
  245.4 11.2 %slice-start = ((s8[4849664]{0:T(1024)(128)(4,1)}), s8[4194304]{0:T(1024)(128)(4,1)S(1)}, s32[]{:S(2)}) async-start(s8[4849664]{0:T(1024)(128)(4,1)} %bitcast.169), calls=%async_computation.12 | async-start | bytes 8388608 | tf_op jit(solution)/shard_map/cond
  248.7 7.9 %copy-start.8 = (f32[1184,512]{1,0:T(8,128)S(1)}, f32[1184,512]{1,0:T(8,128)}, u32[]{:S(2)}) copy-start(f32[1184,512]{1,0:T(8,128)} %copy-done.7) | copy-start | bytes 7274500 | tf_op jit(solution)/shard_map/cond
  248.7 7.9 %slice-start.1 = ((s8[4849664]{0:T(1024)(128)(4,1)}), s8[655360]{0:T(1024)(128)(4,1)S(1)}, s32[]{:S(2)}) async-start(s8[4849664]{0:T(1024)(128)(4,1)} %bitcast.169), calls=%async_computation.13 | async-start | bytes 1310720 | tf_op jit(solution)/shard_map/cond
  264.6 109.7 %reduce-scatter.17.cloned.1.call-start = ((), (), s32[]{:S(2)}) async-start(), calls=%async_computation.10 | async-start | bytes 557056 | tf_op jit(solution)/shard_map/reduce_scatter | solution.py:270
  266.7 168.1 %reduce-scatter.11.cloned.1.call-start = ((), (), s32[]{:S(2)}) async-start(), calls=%async_computation.7 | async-start | bytes 1114112 | tf_op jit(solution)/shard_map/reduce_scatter | solution.py:267
  269.4 234.4 %reduce-scatter.9.cloned.1.call-start = ((), (), s32[]{:S(2)}) async-start(), calls=%async_computation.6 | async-start | bytes 3342336 | tf_op jit(solution)/shard_map/reduce_scatter | solution.py:266
  273.0 306.0 %reduce-scatter.13.cloned.1.call-start = ((), (), s32[]{:S(2)}) async-start(), calls=%async_computation.8 | async-start | bytes 4456448 | tf_op jit(solution)/shard_map/reduce_scatter | solution.py:268
  278.6 376.3 %reduce-scatter.15.cloned.1.call-start = ((), (), s32[]{:S(2)}) async-start(), calls=%async_computation.9 | async-start | bytes 4456448 | tf_op jit(solution)/shard_map/reduce_scatter | solution.py:269
  279.6 83.4 %collective-permute-start = (bf16[1184,128]{1,0:T(8,128)(2,1)S(1)}, bf16[1184,128]{1,0:T(8,128)(2,1)S(1)}, u32[]{:S(2)}, u32[]{:S(2)}) collective-permute-start(bf16[1184,128]{1,0:T(8,128)(2,1)S(1)} %dynamic_slice.155), channel_id=1, source_target_pairs={{0,16},{1,17},{2,18},{3,19},{4,20},{5,21},{6,22},{7,23},{8,24},{9,... | collective-permute-start | bytes 909320 | tf_op jit(solution)/shard_map/ppermute | solution.py:22
  281.0 11.5 %collective-permute-start.9 = (f32[32,1]{0,1:T(1,128)S(1)}, f32[32,1]{0,1:T(1,128)S(1)}, u32[]{:S(2)}, u32[]{:S(2)}) collective-permute-start(f32[32,1]{0,1:T(1,128)S(1)} %fusion.65), channel_id=1, source_target_pairs={{0,16},{16,0},{1,17},{17,1},{2,18},{18,2},{3,19},{19,3},{4,20},{20... | collective-permute-start | bytes 392 | tf_op jit(solution)/shard_map/ppermute | solution.py:26
  282.0 76.1 %collective-permute-start.10 = (f32[32,768]{1,0:T(8,128)S(1)}, f32[32,768]{1,0:T(8,128)S(1)}, u32[]{:S(2)}, u32[]{:S(2)}) collective-permute-start(f32[32,768]{1,0:T(8,128)S(1)} %bitcast_convert_fusion.2), channel_id=1, source_target_pairs={{0,16},{16,0},{1,17},{17,1},{2,18},{18,2},{3,19},{19,3},{4,20},{20... | collective-permute-start | bytes 294920 | tf_op jit(solution)/shard_map/ppermute | solution.py:26
  284.9 67.8 %collective-permute-start.11 = (f32[32,256]{1,0:T(8,128)S(1)}, f32[32,256]{1,0:T(8,128)S(1)}, u32[]{:S(2)}, u32[]{:S(2)}) collective-permute-start(f32[32,256]{1,0:T(8,128)S(1)} %bitcast_convert_fusion.3), channel_id=1, source_target_pairs={{0,16},{16,0},{1,17},{17,1},{2,18},{18,2},{3,19},{19,3},{4,20},{20... | collective-permute-start | bytes 98312 | tf_op jit(solution)/shard_map/ppermute | solution.py:26
  285.8 65.5 %collective-permute-start.14 = (f32[32,128]{1,0:T(8,128)S(1)}, f32[32,128]{1,0:T(8,128)S(1)}, u32[]{:S(2)}, u32[]{:S(2)}) collective-permute-start(f32[32,128]{1,0:T(8,128)S(1)} %bitcast_convert_fusion.4), channel_id=1, source_target_pairs={{0,16},{16,0},{1,17},{17,1},{2,18},{18,2},{3,19},{19,3},{4,20},{20... | collective-permute-start | bytes 49160 | tf_op jit(solution)/shard_map/ppermute | solution.py:26
  345.0 3.8 collective-permute-start.3
  348.8 12.6 %collective-permute-start.12 = (f32[32,1024]{1,0:T(8,128)S(1)}, f32[32,1024]{1,0:T(8,128)S(1)}, u32[]{:S(2)}, u32[]{:S(2)}) collective-permute-start(f32[32,1024]{1,0:T(8,128)S(1)} %bitcast_convert_fusion.1), channel_id=1, source_target_pairs={{0,16},{16,0},{1,17},{17,1},{2,18},{18,2},{3,19},{19,3},{4,20},{20... | collective-permute-start | bytes 393224 | tf_op jit(solution)/shard_map/ppermute | solution.py:26
  351.3 8.4 %collective-permute-start.13 = (f32[128,256]{1,0:T(8,128)S(1)}, f32[128,256]{1,0:T(8,128)S(1)}, u32[]{:S(2)}, u32[]{:S(2)}) collective-permute-start(f32[128,256]{1,0:T(8,128)S(1)} %bitcast_convert_fusion), channel_id=1, source_target_pairs={{0,16},{16,0},{1,17},{17,1},{2,18},{18,2},{3,19},{19,3},{4,20},{20... | collective-permute-start | bytes 393224 | tf_op jit(solution)/shard_map/ppermute | solution.py:26
  352.7 14.9 %collective-permute-start.2 = (bf16[1184,256]{1,0:T(8,128)(2,1)S(1)}, bf16[1184,256]{1,0:T(8,128)(2,1)S(1)}, u32[]{:S(2)}, u32[]{:S(2)}) collective-permute-start(bf16[1184,256]{1,0:T(8,128)(2,1)S(1)} %dynamic_slice.157), channel_id=1, source_target_pairs={{0,16},{1,17},{2,18},{3,19},{4,20},{5,21},{6,22},{7,23},{8,24},{9,... | collective-permute-start | bytes 1818632 | tf_op jit(solution)/shard_map/ppermute | solution.py:22
  375.0 62.0 %collective-permute-start.8 = (f32[32,128]{1,0:T(8,128)S(1)}, f32[32,128]{1,0:T(8,128)S(1)}, u32[]{:S(2)}, u32[]{:S(2)}) collective-permute-start(f32[32,128]{1,0:T(8,128)S(1)} %constant_dynamic-slice_fusion.2), channel_id=1, source_target_pairs={{0,16},{16,0},{1,17},{17,1},{2,18},{18,2},{3,19},{19,3},{4,20},{20... | collective-permute-start | bytes 49160 | tf_op jit(solution)/shard_map/ppermute | solution.py:26
  435.6 3.9 collective-permute-start.5
  504.6 76.9 %collective-permute-start.4 = (f32[32,768]{1,0:T(8,128)S(1)}, f32[32,768]{1,0:T(8,128)S(1)}, u32[]{:S(2)}, u32[]{:S(2)}) collective-permute-start(f32[32,768]{1,0:T(8,128)S(1)} %constant_dynamic-slice_fusion.6), channel_id=1, source_target_pairs={{0,16},{16,0},{1,17},{17,1},{2,18},{18,2},{3,19},{19,3},{4,20},{20... | collective-permute-start | bytes 294920 | tf_op jit(solution)/shard_map/ppermute | solution.py:26
  579.9 77.3 %collective-permute-start.6 = (f32[32,1024]{1,0:T(8,128)S(1)}, f32[32,1024]{1,0:T(8,128)S(1)}, u32[]{:S(2)}, u32[]{:S(2)}) collective-permute-start(f32[32,1024]{1,0:T(8,128)S(1)} %constant_dynamic-slice_fusion.4), channel_id=1, source_target_pairs={{0,16},{16,0},{1,17},{17,1},{2,18},{18,2},{3,19},{19,3},{4,20},{20... | collective-permute-start | bytes 393224 | tf_op jit(solution)/shard_map/ppermute | solution.py:26
  655.8 5.0 collective-permute-start.7
  (43 other events, 167.1 us)
Sparse Core Ops, SparseCore 0:
  264.7 51.1 reduce-scatter.18
  319.5 54.7 reduce-scatter.16
  378.4 56.3 reduce-scatter.10
  438.5 65.2 reduce-scatter.8
  507.5 71.5 reduce-scatter.12
  583.2 71.5 reduce-scatter.14
where the time goes:
time: 677 us; the launch traced here: 669 us
  waiting for transfers between devices  279 us (41%)
  matrix products  117 us (17%)
  local copies, waits for them, and re-layouts  99.3 us (15%)
  blocking collectives  71.8 us (11%)
  other arithmetic  58.6 us (9%)
  starting transfers between devices  22.7 us (3%)
  between operations  20 us (3%)
    reduce_scatter x1, waiting for transfers between devices, local(): lax.psum_scatter(grads[3], 'dp', scatter_dimension=0, tiled=True)  72.9 us
    reduce_scatter x1, waiting for transfers between devices, local(): lax.psum_scatter(grads[4], 'dp', scatter_dimension=0, tiled=True)  71.7 us
    reduce_scatter x1, waiting for transfers between devices, local(): lax.psum_scatter(grads[1], 'dp', scatter_dimension=0, tiled=True)  62.9 us
    reduce_scatter x1, waiting for transfers between devices, local(): lax.psum_scatter(grads[2], 'dp', scatter_dimension=0, tiled=True)  58.3 us
    unnamed x1, blocking collectives  36.9 us
    psum x1, blocking collectives, local(): counts = lax.psum(jnp.sum(table, axis=0), 'dp')  34.9 us
    dot_general x5, matrix products, times_back(): lax.dot_general(left, right, (((1,), (1,)), ((), ())), preferred_element_...  24.3 us
    dot_general x5, matrix products, inner_rows(): lax.dot_general(left, right, (((0,), (0,)), ((), ())), preferred_element_...  21.2 us
  transfers between devices with their start and end apart: 21, of which 9 were waited for; matrix products, arithmetic and copies ran while one was open for 9% of the time, Pallas kernels for 0%

commit v1 on v0

v1 whole, which is shorter than its diff:
```python
import functools

import jax
import jax.numpy as jnp
from jax import lax
from jax.experimental import pallas as pl
from jax.experimental.pallas import tpu as pltpu
from jax.sharding import PartitionSpec as P

F32 = jnp.float32
BF16 = jnp.bfloat16
MESH = pl.DeviceIdType.MESH

HEAD_DIM = 64
L = 296
LP = 304
TASKS = 32
EPSILON = 1e-06
DISCOUNT = 0.98
SOFT_RATE = 0.2
SCORE_SCALE = 0.125
NEG_LARGE = -1000000000.0
LOWEST = -1e30

BLOCKS = ((0, 128, 128), (128, 128, 256), (256, 48, 304))


def dot_nn(a, b):
    return lax.dot_general(a, b, (((1,), (0,)), ((), ())), preferred_element_type=F32)


def dot_nt(a, b):
    return lax.dot_general(a, b, (((1,), (1,)), ((), ())), preferred_element_type=F32)


def dot_tn(a, b):
    return lax.dot_general(a, b, (((0,), (0,)), ((), ())), preferred_element_type=F32)


def dot_tt(a, b):
    return lax.dot_general(a, b, (((0,), (1,)), ((), ())), preferred_element_type=F32)


def inverse_rms(values):
    return lax.rsqrt(jnp.mean(values * values, axis=-1, keepdims=True) + EPSILON)


def gelu_and_slope(u):
    c = 0.7978845608028654
    square = u * u
    t = jnp.tanh(u * (c + (c * 0.044715) * square))
    half = 0.5 * t + 0.5
    slope = half + (u * (0.5 - 0.5 * t * t)) * (c + (3 * c * 0.044715) * square)
    return u * half, slope


def lane_halves(a):
    lane = lax.broadcasted_iota(jnp.int32, (1, 2 * HEAD_DIM), 1)
    zero = jnp.zeros((), a.dtype)
    return jnp.where(lane < HEAD_DIM, a, zero), jnp.where(lane >= HEAD_DIM, a, zero)


def rows_of(ref, first, width):
    value = ref[:, :, first : first + width]
    return value.reshape(value.shape[0] * value.shape[1], width)


class Names:
    pass


def forward_sequence(n, s, d):
    x = n.x[s].astype(F32)
    normed = (x * inverse_rms(x) * n.gains[0:1, :]).astype(BF16)
    n.normed_one[s] = normed
    for first in range(0, 3 * d, 256):
        n.qkv[s, :, first : first + 256] = dot_nn(
            normed, n.w_qkv[:, first : first + 256]
        ).astype(BF16)
    corner = lax.broadcasted_iota(jnp.int32, (128, 128), 0) >= lax.broadcasted_iota(
        jnp.int32, (128, 128), 1
    )
    for pair in range(d // 128):
        at = 128 * pair
        queries = lane_halves(n.qkv[s, :, at : at + 128] * jnp.array(SCORE_SCALE, BF16))
        keys = n.qkv[s, :, d + at : d + at + 128]
        values = lane_halves(n.qkv[s, :, 2 * d + at : 2 * d + at + 128])
        for block, (first, rows, seen) in enumerate(BLOCKS):
            mixed = None
            for head in range(2):
                raw = dot_nt(queries[head][first : first + rows], keys[:seen])
                diagonal = jnp.where(corner[:rows, :rows], raw[:, first:], NEG_LARGE)
                scores = jnp.concatenate([raw[:, :first], diagonal], axis=1) if first else diagonal
                largest = jnp.max(scores, axis=-1, keepdims=True)
                raised = jnp.exp(scores - largest)
                totals = jnp.sum(raised, axis=-1, keepdims=True)
                probs = (raised * (1.0 / totals)).astype(BF16)
                n.probs[block][s, 2 * pair + head] = probs
                part = dot_nn(probs, values[head][:seen])
                mixed = part if mixed is None else mixed + part
            n.attended[s, first : first + rows, at : at + 128] = mixed.astype(BF16)
    middle = x + dot_nn(n.attended[s], n.w_out[...])
    n.middle[s] = middle
    normed = (middle * inverse_rms(middle) * n.gains[1:2, :]).astype(BF16)
    n.normed_two[s] = normed
    ff = n.w_up.shape[1]
    for first in range(0, ff, 256):
        active, slope = gelu_and_slope(dot_nn(normed, n.w_up[:, first : first + 256]))
        n.active[s, :, first : first + 256] = active.astype(BF16)
        n.slope[s, :, first : first + 256] = slope.astype(BF16)
    final_low = (n.middle[s] + dot_nn(n.active[s], n.w_down[...])).astype(BF16)
    n.final_low[s] = final_low
    n.q_rows[s] = dot_nn(final_low, n.w_head[...]).astype(BF16)
    q_columns = dot_tt(n.w_head[...], final_low)
    bins = lax.broadcasted_iota(jnp.int32, q_columns.shape, 0)
    chosen = n.aux[s, 0:1, :].astype(jnp.int32)
    n.picked[pl.ds(s, 1), :] = jnp.sum(
        jnp.where(bins == chosen, q_columns, 0.0), axis=0, keepdims=True
    )
    n.tops[pl.ds(s, 1), :] = jnp.max(q_columns, axis=0, keepdims=True)


def backward_ffn(n, s):
    bins = lax.broadcasted_iota(jnp.int32, (n.w_head.shape[1], LP), 0)
    chosen = n.aux[s, 0:1, :].astype(jnp.int32)
    grad_q = jnp.where(bins == chosen, n.coef[pl.ds(s, 1), :], 0.0).astype(BF16)
    n.grad_q[s] = grad_q
    grad_final = dot_tt(grad_q, n.w_head[...])
    grad_ffn = grad_final.astype(BF16)
    n.grad_ffn[s] = grad_ffn
    ff = n.w_up.shape[1]
    for first in range(0, ff, 256):
        grad_active = dot_nt(grad_ffn, n.w_down[first : first + 256, :])
        n.slope[s, :, first : first + 256] = (
            grad_active * n.slope[s, :, first : first + 256].astype(F32)
        ).astype(BF16)
    grad_two = dot_nt(n.slope[s], n.w_up[...])
    middle = n.middle[s]
    inverse = inverse_rms(middle)
    normal = middle * inverse
    n.gain_sums[1] += jnp.sum((grad_two * normal).reshape(LP // 8, 8, -1), axis=0)
    inner = grad_two * n.gains[1:2, :]
    grad_middle = grad_final + inverse * (
        inner - normal * jnp.mean(inner * normal, axis=-1, keepdims=True)
    )
    n.middle[s] = grad_middle
    grad_branch = grad_middle.astype(BF16)
    n.grad_branch[s] = grad_branch
    n.grad_mixed[s] = dot_nt(grad_branch, n.w_out[...]).astype(BF16)


def backward_attention(n, s, d):
    lane = lax.broadcasted_iota(jnp.int32, (1, 128), 1)
    for pair in range(d // 128):
        at = 128 * pair
        values = n.qkv[s, :, 2 * d + at : 2 * d + at + 128]
        grad_mixed = n.grad_mixed[s, :, at : at + 128]
        product = n.attended[s, :, at : at + 128].astype(F32) * grad_mixed.astype(F32)
        centres = (
            jnp.sum(jnp.where(lane < HEAD_DIM, product, 0.0), axis=-1, keepdims=True),
            jnp.sum(jnp.where(lane >= HEAD_DIM, product, 0.0), axis=-1, keepdims=True),
        )
        queries = lane_halves(n.qkv[s, :, at : at + 128])
        keys = lane_halves(n.qkv[s, :, d + at : d + at + 128])
        grads = lane_halves(grad_mixed)
        grad_keys = [None] * 3
        grad_values = [None] * 3
        for block, (first, rows, seen) in enumerate(BLOCKS):
            grad_queries = None
            for head in range(2):
                probs = n.probs[block][s, 2 * pair + head]
                here = grads[head][first : first + rows]
                grad_probs = dot_nt(here, values[:seen])
                grad_scores = (
                    probs.astype(F32) * (grad_probs - centres[head][first : first + rows])
                ).astype(BF16)
                part = dot_nn(grad_scores, keys[head][:seen])
                grad_queries = part if grad_queries is None else grad_queries + part
                of_values = dot_tn(probs, here)
                of_keys = dot_tn(grad_scores, queries[head][first : first + rows])
                for i, start in enumerate((0, 128, 256)):
                    if start < seen:
                        end = min(start + 128, seen)
                        piece = of_values[start:end]
                        grad_values[i] = piece if grad_values[i] is None else grad_values[i] + piece
                        piece = of_keys[start:end]
                        grad_keys[i] = piece if grad_keys[i] is None else grad_keys[i] + piece
            n.qkv[s, first : first + rows, at : at + 128] = (grad_queries * SCORE_SCALE).astype(
                BF16
            )
        for i, (first, rows, _) in enumerate(BLOCKS):
            n.qkv[s, first : first + rows, d + at : d + at + 128] = (
                grad_keys[i] * SCORE_SCALE
            ).astype(BF16)
            n.qkv[s, first : first + rows, 2 * d + at : 2 * d + at + 128] = grad_values[i].astype(
                BF16
            )
    grad_one = dot_nt(n.qkv[s], n.w_qkv[...])
    x = n.x[s].astype(F32)
    inverse = inverse_rms(x)
    normal = x * inverse
    n.gain_sums[0] += jnp.sum((grad_one * normal).reshape(LP // 8, 8, -1), axis=0)
    inner = grad_one * n.gains[0:1, :]
    n.grad_states[s] = (
        n.middle[s]
        + inverse * (inner - normal * jnp.mean(inner * normal, axis=-1, keepdims=True))
    ).astype(BF16)


TENSORS = ("down", "up", "out", "head", "qkv")
SEMAPHORES = 96


def layer_kernel(names, data_count, inside, *refs):
    n = Names()
    for name, ref in zip(names, refs):
        setattr(n, name, ref)
    n.probs = (n.probs_0, n.probs_1, n.probs_2)
    d = n.x.shape[2]
    ff = n.w_up.shape[1]
    seq_count = n.x.shape[0]

    me_pair = lax.axis_index("pair")
    me = lax.axis_index("dp")
    other = 1 - me_pair
    core = me % 2
    row = (me // 2) % 2
    low = (me // 4) % 2
    high = me // 8
    sibling = (me_pair, me + 1 - 2 * core)
    beside = (me_pair, me + 2 - 4 * row)
    near = (me_pair, me + 4 - 8 * low)
    partner = (other, me)
    quarter = me // 4

    def at_quarter(which, pair):
        return (pair, me + 4 * (which - quarter))

    def at_mixed(which, pair):
        return (pair, me + 8 * (which // 2 - high) + 2 * (which % 2 - row))

    used = [0]
    sent = []

    def slot():
        used[0] += 1
        return used[0] - 1

    def copy(src, dst, sem, device):
        return pltpu.make_async_remote_copy(
            src_ref=src,
            dst_ref=dst,
            send_sem=n.send_sem.at[sem],
            recv_sem=n.recv_sem.at[sem],
            device_id=device,
            device_id_type=MESH,
        )

    online = me_pair == 0

    barrier = pltpu.get_barrier_semaphore()
    friends = [partner]
    if inside:
        friends += [sibling, beside]
        for offset in range(1, 4):
            place = (quarter + offset) % 4
            friends += [at_quarter(place, me_pair), at_quarter(place, other)]
        friends += [
            (pair, me + 8 * (1 - 2 * high) + 2 * (1 - 2 * row)) for pair in (me_pair, other)
        ]
        friends += [(other, beside[1])]
    for friend in friends:
        pl.semaphore_signal(barrier, inc=1, device_id=friend, device_id_type=MESH)

    weight_refs = (n.w_qkv, n.w_out, n.w_up, n.w_down, n.w_head)
    if inside:
        theirs = (n.their_qkv, n.their_out, n.their_up, n.their_down, n.their_head)

    def piece_of(ref, half):
        height = ref.shape[0] // data_count
        width = ref.shape[1] // 2
        return (
            pl.ds(pl.multiple_of(me * height, height), height),
            pl.ds(pl.multiple_of(half * width, width), width),
        )

    weight_sems = [slot() for _ in weight_refs]

    def weight_copy(i):
        return copy(weight_refs[i].at[piece_of(weight_refs[i], other)], theirs[i], weight_sems[i], partner)

    gains_sem = slot()

    def gains_copy():
        return copy(n.gains, n.their_gains, gains_sem, partner)

    count_core, count_row = slot(), slot()
    count_far = [slot() for _ in range(3)]

    def count_copy(step, offset=0):
        if step == 0:
            return copy(n.count_out.at[0], n.count_in.at[0], count_core, sibling)
        if step == 1:
            return copy(n.count_out.at[1], n.count_in.at[1], count_row, beside)
        place = (quarter + offset) % 4
        return copy(
            n.count_out.at[2],
            n.count_in.at[1 + offset],
            count_far[offset - 1],
            at_quarter(place, me_pair),
        )

    n.gain_sums[...] = jnp.zeros_like(n.gain_sums)

    @pl.loop(0, seq_count)
    def _(s):
        forward_sequence(n, s, d)

        @pl.when(s == 0)
        def _():
            pl.semaphore_wait(barrier, len(friends))
            if not inside:
                return
            n.count_out[0] = jnp.broadcast_to(
                jnp.sum(n.table[...], axis=0, keepdims=True), (8, 128)
            )
            count_copy(0).start()
            for i in range(len(weight_refs)):
                weight_copy(i).start()
            gains_copy().start()

        if not inside:
            return

        @pl.when(s == 1)
        def _():
            count_copy(0).wait()
            n.count_out[1] = n.count_out[0] + n.count_in[0]
            count_copy(1).start()

        @pl.when(s == 2)
        def _():
            count_copy(1).wait()
            n.count_out[2] = n.count_out[1] + n.count_in[1]
            for offset in range(1, 4):
                count_copy(2, offset).start()

    lane = lax.broadcasted_iota(jnp.int32, (8, LP), 1)
    seq = lax.broadcasted_iota(jnp.int32, (8, LP), 0)
    real = jnp.logical_and(lane < L, seq < seq_count)
    tops = n.tops[...]
    aims_sem = slot()
    q_sem = slot()
    state_sems = [slot() for _ in range(1)]
    state_sems = state_sems + [slot() for _ in range(seq_count - 1)]

    def aims_copy():
        return copy(n.aims_out, n.aims_in, aims_sem, partner)

    def q_copy():
        return copy(n.q_rows.at[:, :, pl.ds(128, 128)], n.q_half, q_sem, partner)

    def state_copy(s):
        return copy(
            n.grad_states.at[s, :, pl.ds(d // 2, d // 2)],
            n.state_half.at[s],
            state_sems[0] + s,
            partner,
        )

    @pl.when(jnp.logical_not(online))
    def _():
        reward = jnp.concatenate([n.aux[s, 1:2, :] for s in range(seq_count)] * 2, axis=0)
        finished = jnp.concatenate([n.aux[s, 2:3, :] for s in range(seq_count)] * 2, axis=0)
        n.aims_out[...] = reward + DISCOUNT * (1.0 - finished) * tops
        aims_copy().start()

    @pl.when(online)
    def _():
        q_copy().start()

    if inside:
        for i in range(len(weight_refs)):
            weight_copy(i).wait()
            mine = weight_refs[i][piece_of(weight_refs[i], me_pair)].astype(F32)
            received = theirs[i][...].astype(F32)
            first = jnp.where(online, mine, received)
            second = jnp.where(online, received, mine)
            (n.new_qkv, n.new_out, n.new_up, n.new_down, n.new_head)[i][...] = second + SOFT_RATE * (
                first - second
            )
        gains_copy().wait()
        first = jnp.where(online, n.gains[...], n.their_gains[...])
        second = jnp.where(online, n.their_gains[...], n.gains[...])
        n.new_gains[...] = second + SOFT_RATE * (first - second)

        for offset in range(1, 4):
            count_copy(2, offset).wait()
        counts = n.count_out[2] + n.count_in[2] + n.count_in[3] + n.count_in[4]
    else:
        counts = n.counts[...]
    seq_weight = (seq_count * data_count) / (
        TASKS * jnp.sum(n.table[...] * counts, axis=1, keepdims=True)
    )

    stat_core, stat_row = slot(), slot()
    stat_far = [slot() for _ in range(7)]
    stat_row_id = lax.broadcasted_iota(jnp.int32, (8, 128), 0)
    stat_lane = lax.broadcasted_iota(jnp.int32, (8, 128), 1)

    def stat_copy(step, k=0):
        if step == 0:
            return copy(n.stat_out.at[0], n.stat_in.at[0], stat_core, sibling)
        if step == 1:
            return copy(n.stat_out.at[1], n.stat_in.at[1], stat_row, beside)
        place = (quarter + (k + 1) % 4) % 4
        pair = me_pair if k < 3 else other
        return copy(n.stat_out.at[2], n.stat_in.at[2 + k], stat_far[k], at_quarter(place, pair))

    def stat_join(a, b):
        return jnp.where(stat_row_id == 1, jnp.maximum(a, b), a + b)

    def stat_first(loss):
        total = jnp.sum(jnp.where(real, tops, 0.0))
        best = jnp.max(jnp.where(real, tops, LOWEST))
        sums = jnp.where(
            stat_lane == 0, loss, jnp.where(stat_lane == 1 + me_pair, total, 0.0)
        )
        bests = jnp.where(stat_lane == me_pair, best, LOWEST)
        n.stat_out[0] = jnp.where(
            stat_row_id == 0, sums, jnp.where(stat_row_id == 1, bests, 0.0)
        )
        if inside:
            stat_copy(0).start()

    def stat_second():
        if not inside:
            return
        stat_copy(0).wait()
        n.stat_out[1] = stat_join(n.stat_out[0], n.stat_in[0])
        stat_copy(1).start()

    def stat_third():
        if not inside:
            return
        stat_copy(1).wait()
        n.stat_out[2] = stat_join(n.stat_out[1], n.stat_in[1])
        for k in range(7):
            stat_copy(2, k).start()

    step_sems = {}
    for name in TENSORS:
        step_sems[name] = (slot(), slot(), [slot() for _ in range(7)])
    along = {"down": "row", "up": "low", "out": "row", "head": "row", "qkv": "row"}
    gain_sems = (slot(), slot(), [slot() for _ in range(7)])

    def core_start(name):
        if inside:
            core_copy(name).start()

    def core_copy(name):
        return copy(
            getattr(n, "g_" + name).at[:, :, :, 1 - core],
            getattr(n, "r1_" + name),
            step_sems[name][0],
            sibling,
        )

    def axis_copy(name):
        r1, r2 = getattr(n, "r1_" + name), getattr(n, "r2_" + name)
        if along[name] == "row":
            return copy(r1.at[:, :, 1 - row], r2, step_sems[name][1], beside)
        return copy(r1.at[:, 1 - low], r2, step_sems[name][1], near)

    def half_of(name, half):
        height, width = getattr(n, "r2_" + name).shape[2:]
        if name == "down":
            return (pl.ds(half * (height // 2), height // 2), slice(None))
        return (slice(None), pl.ds(half * (width // 2), width // 2))

    def far_copy(name, k):
        r2, r3 = getattr(n, "r2_" + name), getattr(n, "r3_" + name)
        offset = (k + 1) % 4
        pair = 0 if k < 3 else 1
        if along[name] == "row":
            place = (quarter + offset) % 4
            device = at_quarter(place, pair)
        else:
            place = (2 * high + row + offset) % 4
            device = at_mixed(place, pair)
        return copy(
            r2.at[(place // 2, place % 2) + half_of(name, pair)],
            r3.at[offset],
            step_sems[name][2][k],
            device,
        )

    def core_done(name):
        if not inside:
            return
        core_copy(name).wait()
        g, r1 = getattr(n, "g_" + name), getattr(n, "r1_" + name)
        for i in range(2):
            for j in range(2):
                for k in range(2):
                    r1[i, j, k] = (g[i, j, k, core].astype(F32) + r1[i, j, k].astype(F32)).astype(
                        BF16
                    )
        axis_copy(name).start()

    def axis_done(name):
        if not inside:
            return
        axis_copy(name).wait()
        r1, r2 = getattr(n, "r1_" + name), getattr(n, "r2_" + name)
        for i in range(2):
            for j in range(2):
                mine = r1[i, j, row] if along[name] == "row" else r1[i, low, j]
                r2[i, j] = (mine.astype(F32) + r2[i, j].astype(F32)).astype(BF16)
        for k in range(7):
            far_copy(name, k).start()

    def owner_online(name):
        if not inside:
            return
        r2, r3 = getattr(n, "r2_" + name), getattr(n, "r3_" + name)
        place = quarter if along[name] == "row" else 2 * high + row
        total = r2[(place // 2, place % 2) + half_of(name, 0)].astype(F32)
        for k in range(3):
            far_copy(name, k).wait_recv()
            total += r3[k + 1].astype(F32)
        getattr(n, "grad_" + name)[...] = total

    def owner_target(name):
        if not inside:
            return
        r3 = getattr(n, "r3_" + name)
        total = None
        for k in range(3, 7):
            far_copy(name, k).wait_recv()
            part = r3[(k + 1) % 4].astype(F32)
            total = part if total is None else total + part
        getattr(n, "grad_" + name)[...] = total

    def gain_copy(step, k=0):
        if step == 0:
            return copy(n.gain_out.at[0], n.gain_in.at[0], gain_sems[0], sibling)
        if step == 1:
            return copy(n.gain_out.at[1], n.gain_in.at[1], gain_sems[1], beside)
        offset = (k + 1) % 4
        pair = 0 if k < 3 else 1
        return copy(
            n.gain_out.at[2],
            n.gain_in.at[2 + offset],
            gain_sems[2][k],
            at_quarter((quarter + offset) % 4, pair),
        )

    @pl.when(online)
    def _():
        aims_copy().wait_recv()
        differ = n.picked[...] - n.aims_in[...]
        weighted = jnp.where(real, seq_weight * differ, 0.0)
        n.coef[...] = weighted
        stat_first(jnp.sum(0.5 * weighted * jnp.where(real, differ, 0.0)))

        @pl.loop(0, seq_count)
        def _(s):
            backward_ffn(n, s)

        stat_second()
        grad_ffn = rows_of(n.grad_ffn, 0, d)

        @pl.loop(0, ff // 256)
        def _(j):
            columns = pl.ds(pl.multiple_of(j * 256, 256), 256)
            value = dot_tn(grad_ffn, n.active[:, :, columns].reshape(seq_count * LP, 256))
            for c in range(2):
                n.g_down[j // 4, (j // 2) % 2, j % 2, c] = value[:, 128 * c : 128 * c + 128].astype(
                    BF16
                )

        core_start("down")
        normed_two = rows_of(n.normed_two, 0, d)

        @pl.loop(0, ff // 256)
        def _(j):
            columns = pl.ds(pl.multiple_of(j * 256, 256), 256)
            value = dot_tn(normed_two, n.slope[:, :, columns].reshape(seq_count * LP, 256))
            n.g_up[:, :, :, :, :, columns] = value.astype(BF16).reshape(2, 2, 2, 2, d // 16, 256)

        core_start("up")
        core_done("down")
        value = dot_tn(rows_of(n.attended, 0, d), rows_of(n.grad_branch, 0, d))
        n.g_out[...] = value.astype(BF16).reshape(n.g_out.shape)
        value = None
        for s in range(seq_count):
            part = dot_nn(n.grad_q[s], n.final_low[s])
            value = part if value is None else value + part
        n.g_head[...] = jnp.transpose(value).astype(BF16).reshape(n.g_head.shape)
        core_start("out")
        core_start("head")
        core_done("up")

        @pl.loop(0, seq_count)
        def _(s):
            backward_attention(n, s, d)
            state_copy(s).start()

            @pl.when(s == 0)
            def _():
                core_done("out")
                core_done("head")
                stat_third()

            @pl.when(s == 2)
            def _():
                axis_done("down")

        n.gain_out[0, 0:1, :] = jnp.sum(n.gain_sums[0], axis=0, keepdims=True)
        n.gain_out[0, 1:2, :] = jnp.sum(n.gain_sums[1], axis=0, keepdims=True)
        n.gain_out[0, 2:8, :] = jnp.zeros((6, d), F32)
        if inside:
            gain_copy(0).start()
        normed_one = rows_of(n.normed_one, 0, d)

        @pl.loop(0, 3 * d // 256)
        def _(j):
            columns = pl.ds(pl.multiple_of(j * 256, 256), 256)
            value = dot_tn(normed_one, n.qkv[:, :, columns].reshape(seq_count * LP, 256))
            n.g_qkv[:, :, :, :, :, columns] = value.astype(BF16).reshape(2, 2, 2, 2, d // 16, 256)

        core_start("qkv")
        axis_done("up")
        core_done("qkv")
        if inside:
            gain_copy(0).wait()
            n.gain_out[1] = n.gain_out[0] + n.gain_in[0]
            gain_copy(1).start()
        axis_done("out")
        axis_done("head")
        owner_online("down")
        if inside:
            gain_copy(1).wait()
            n.gain_out[2] = n.gain_out[1] + n.gain_in[1]
            for k in range(7):
                gain_copy(2, k).start()
        owner_online("up")
        axis_done("qkv")
        for s in range(seq_count):
            n.state_out[s] = n.grad_states[s, :, : d // 2]
        n.q_out[...] = n.q_rows[:, :, :128]
        owner_online("out")
        owner_online("head")
        if inside:
            total = n.gain_out[2]
            for k in range(3):
                gain_copy(2, k).wait_recv()
                total += n.gain_in[3 + k]
            n.grad_gains[...] = total
        else:
            n.grad_gains[...] = n.gain_out[0]
        owner_online("qkv")
        q_copy().wait_send()
        for s in range(seq_count):
            state_copy(s).wait_send()
        if inside:
            for k in range(7):
                for name in TENSORS:
                    far_copy(name, k).wait_send()
                gain_copy(2, k).wait_send()

    @pl.when(jnp.logical_not(online))
    def _():
        stat_first(0.0)
        stat_second()
        stat_third()
        q_copy().wait_recv()
        n.q_out[...] = n.q_half[...]
        for name in TENSORS[:4]:
            owner_target(name)
        for s in range(seq_count):
            state_copy(s).wait_recv()
            n.state_out[s] = n.state_half[s]
        if inside:
            total = None
            for k in range(3, 7):
                gain_copy(2, k).wait_recv()
                part = n.gain_in[2 + (k + 1) % 4]
                total = part if total is None else total + part
            n.grad_gains[...] = total
        owner_target("qkv")
        aims_copy().wait_send()

    if inside:
        for k in range(7):
            stat_copy(2, k).wait()
        joined = n.stat_out[2]
        for k in range(7):
            joined = stat_join(joined, n.stat_in[2 + k])
        n.stats[...] = joined
    else:
        n.stats[...] = n.stat_out[0]
    assert used[0] <= SEMAPHORES


def pad_rows(values, seq_count):
    shaped = values.reshape((seq_count, L) + values.shape[1:])
    return jnp.pad(shaped, ((0, 0), (0, LP - L)) + ((0, 0),) * (shaped.ndim - 2))


def add_outside(out, params, pair_index, data_index, data_count):
    online = pair_index == 0
    other = 1 - pair_index

    def half(matrix, which):
        width = matrix.shape[1] // 2
        return lax.dynamic_slice_in_dim(matrix, which * width, width, 1)

    def piece(matrix, which):
        height = matrix.shape[0] // data_count
        return half(lax.dynamic_slice_in_dim(matrix, data_index * height, height, 0), which)

    def swapped(value):
        return lax.ppermute(value, "pair", [(0, 1), (1, 0)])

    for name in TENSORS:
        grad = out["g_" + name].astype(F32)
        grad = grad.reshape((16,) + grad.shape[4:])
        if name == "down":
            grad = jnp.swapaxes(grad, 1, 2)
        grad = lax.psum_scatter(
            grad.reshape(-1, grad.shape[2]), "dp", scatter_dimension=0, tiled=True
        )
        received = swapped(half(grad, other))
        out["grad_" + name] = jnp.where(online, half(grad, pair_index), received)
    gains = lax.psum(out["grad_gains"], "dp")
    out["grad_gains"] = jnp.where(online, gains, swapped(gains))
    for name, weight in zip(("gains", "qkv", "out", "up", "down", "head"), params):
        if name == "gains":
            weight = jnp.pad(weight.T, ((0, 6), (0, 0)))
            mine, received = weight.astype(F32), swapped(weight).astype(F32)
        else:
            mine = piece(weight, pair_index).astype(F32)
            received = swapped(piece(weight, other)).astype(F32)
        first, second = jnp.where(online, mine, received), jnp.where(online, received, mine)
        out["new_" + name] = second + SOFT_RATE * (first - second)
    sums = lax.psum(out["stats"][0:1], ("pair", "dp"))
    bests = lax.pmax(out["stats"][1:2], ("pair", "dp"))
    out["stats"] = jnp.concatenate([sums, bests])


def local(
    states, norm_gains, w_qkv, w_out, w_up, w_down, w_head, task_ids, chosen, reward, finished
):
    pair_index = lax.axis_index("pair")
    data_index = lax.axis_index("dp")
    data_count = lax.axis_size("dp")
    row_count, d = states.shape[1:]
    ff = w_up.shape[2]
    bin_count = w_head.shape[2]
    seq_count = row_count // L

    x = pad_rows(states[0], seq_count)
    gains = jnp.pad(norm_gains[0].astype(F32).T, ((0, 6), (0, 0)))
    aux = jnp.stack([pad_rows(a, seq_count).astype(F32) for a in (chosen, reward, finished)], axis=1)
    aux = jnp.pad(aux, ((0, 0), (0, 5), (0, 0)))
    table = (task_ids[:, None] == jnp.arange(128, dtype=jnp.int32)[None, :]).astype(F32)
    table = jnp.pad(table, ((0, 8 - seq_count), (0, 0)))

    inside = data_count == 16
    heads = d // HEAD_DIM
    rows = (seq_count, LP, d)
    inputs = dict(
        x=x,
        gains=gains,
        w_qkv=w_qkv[0],
        w_out=w_out[0],
        w_up=w_up[0],
        w_down=w_down[0],
        w_head=w_head[0],
        aux=aux,
        table=table,
    )
    if not inside:
        inputs["counts"] = jnp.broadcast_to(
            lax.psum(jnp.sum(table, axis=0, keepdims=True), "dp"), (8, 128)
        )
    piece = {
        "qkv": (d // 16, 3 * d),
        "out": (d // 16, d),
        "up": (d // 16, ff),
        "head": (d // 16, bin_count),
        "down": (d, ff // 16),
    }
    halves = {
        name: (shape[0] // 2, shape[1]) if name == "down" else (shape[0], shape[1] // 2)
        for name, shape in piece.items()
    }
    new_shapes = dict(halves, down=(ff // 16, d // 2))
    outputs = dict(
        q_out=((seq_count, LP, bin_count // 2), BF16),
        state_out=((seq_count, LP, d // 2), BF16),
        grad_gains=((8, d), F32),
        new_gains=((8, d), F32),
        stats=((8, 128), F32),
    )
    for name in TENSORS:
        if inside:
            outputs["grad_" + name] = (halves[name], F32)
            outputs["new_" + name] = (new_shapes[name], F32)
        else:
            outputs["g_" + name] = ((2, 2, 2, 2) + piece[name], BF16)
    scratch = dict(
        normed_one=(rows, BF16),
        qkv=((seq_count, LP, 3 * d), BF16),
        probs_0=((seq_count, heads) + (BLOCKS[0][1], BLOCKS[0][2]), BF16),
        probs_1=((seq_count, heads) + (BLOCKS[1][1], BLOCKS[1][2]), BF16),
        probs_2=((seq_count, heads) + (BLOCKS[2][1], BLOCKS[2][2]), BF16),
        attended=(rows, BF16),
        middle=(rows, F32),
        normed_two=(rows, BF16),
        active=((seq_count, LP, ff), BF16),
        slope=((seq_count, LP, ff), BF16),
        final_low=(rows, BF16),
        q_rows=((seq_count, LP, bin_count), BF16),
        q_half=((seq_count, LP, bin_count // 2), BF16),
        picked=((8, LP), F32),
        tops=((8, LP), F32),
        coef=((8, LP), F32),
        aims_out=((8, LP), F32),
        aims_in=((8, LP), F32),
        grad_q=((seq_count, bin_count, LP), BF16),
        grad_ffn=(rows, BF16),
        grad_branch=(rows, BF16),
        grad_mixed=(rows, BF16),
        grad_states=(rows, BF16),
        state_half=((seq_count, LP, d // 2), BF16),
        gain_sums=((2, 8, d), F32),
        gain_out=((3, 8, d), F32),
        gain_in=((6, 8, d), F32),
        count_out=((3, 8, 128), F32),
        count_in=((5, 8, 128), F32),
        stat_out=((3, 8, 128), F32),
        stat_in=((9, 8, 128), F32),
        their_gains=((8, d), F32),
    )
    for name in TENSORS if inside else ():
        scratch["g_" + name] = ((2, 2, 2, 2) + piece[name], BF16)
        scratch["r1_" + name] = ((2, 2, 2) + piece[name], BF16)
        scratch["r2_" + name] = ((2, 2) + piece[name], BF16)
        scratch["r3_" + name] = ((4,) + halves[name], BF16)
        scratch["their_" + name] = (new_shapes[name], BF16)
    names = list(inputs) + list(outputs) + list(scratch) + ["send_sem", "recv_sem"]
    in_vmem = pl.BlockSpec(memory_space=pltpu.VMEM)
    raw = pl.pallas_call(
        functools.partial(layer_kernel, names, data_count, inside),
        out_shape=[jax.ShapeDtypeStruct(shape, dtype) for shape, dtype in outputs.values()],
        in_specs=[in_vmem] * len(inputs),
        out_specs=[in_vmem] * len(outputs),
        scratch_shapes=[pltpu.VMEM(shape, dtype) for shape, dtype in scratch.values()]
        + [pltpu.SemaphoreType.DMA((SEMAPHORES,)), pltpu.SemaphoreType.DMA((SEMAPHORES,))],
        compiler_params=pltpu.CompilerParams(
            collective_id=0, has_side_effects=True, vmem_limit_bytes=64 * 1024 * 1024 - 65536
        ),
        name="layer",
    )(*inputs.values())
    out = dict(zip(outputs, raw))
    token_total = row_count * data_count

    def unpad(values):
        return values[:, :L].reshape((row_count,) + values.shape[2:])

    if not inside:
        params = (norm_gains[0], w_qkv[0], w_out[0], w_up[0], w_down[0], w_head[0])
        add_outside(out, params, pair_index, data_index, data_count)
    height = d // data_count

    def gains_piece(values):
        return lax.dynamic_slice(values, (pair_index, data_index * height), (1, height)).reshape(
            height, 1
        )

    stats = jnp.stack(
        [
            out["stats"][0, 0] / token_total,
            out["stats"][0, 1] / token_total,
            out["stats"][1, 0],
            out["stats"][0, 2] / token_total,
            out["stats"][1, 1],
        ]
    )
    return (
        unpad(out["q_out"]),
        unpad(out["state_out"]),
        gains_piece(out["grad_gains"]),
        out["grad_qkv"],
        out["grad_out"],
        out["grad_up"],
        out["grad_down"].T if inside else out["grad_down"],
        out["grad_head"],
        gains_piece(out["new_gains"]),
        out["new_qkv"],
        out["new_out"],
        out["new_up"],
        out["new_down"],
        out["new_head"],
        stats,
    )


def solution(mesh):
    placed = (
        P("pair", "dp", None),
        P("pair", None, None),
        P("pair", None, None),
        P("pair", None, None),
        P("pair", None, None),
        P("pair", None, None),
        P("pair", None, None),
        P("dp"),
        P("dp"),
        P("dp"),
        P("dp"),
    )
    return jax.shard_map(
        local,
        mesh=mesh,
        in_specs=placed,
        out_specs=(P("dp", "pair"),) * 14 + (P(),),
        check_vma=False,
    )
```

time: 677 us -> 139 us (0.21); the launches traced: 669 us -> 138 us
  waiting for transfers between devices: 279 us -> 0 us
  matrix products: 117 us -> 0 us
  Pallas kernels: 0 us -> 116 us
  local copies, waits for them, and re-layouts: 99.3 us -> 17.5 us
  blocking collectives: 71.8 us -> 0 us
  other arithmetic: 58.6 us -> 1.95 us
  starting transfers between devices: 22.7 us -> 0 us
  between operations: 20 us -> 2.75 us
    reduce_scatter x5 -> x0, waiting for transfers between devices: 270 us -> none  [the longest x1 72.9 us: local(): lax.psum_scatter(grads[3], 'dp', scatter_dimension=0, tiled=True)]
    dot_general x22 -> x0, matrix products: 117 us -> none  [the longest x5 24.3 us: times_back(): lax.dot_general(left, right, (((1,), (1,)), ((), ())), preferred_element_...]
    pallas_call x0 -> x1, Pallas kernels: none -> 116 us  [local(): pl.pallas_call(functools.partial(layer_kernel, names, data_count, inside)...]
    unnamed x1 -> x0, blocking collectives: 36.9 us -> none
    psum x1 -> x0, blocking collectives: 34.9 us -> none  [local(): counts = lax.psum(jnp.sum(table, axis=0), 'dp')]
    cond x78 -> x0, local copies, waits for them, and re-layouts: 24.7 us -> none  [the longest x5 19.1 us: local(): grad_tokens, grads = lax.cond(online, run_back, skip_back)]
    ppermute x15 -> x0, starting transfers between devices: 22.5 us -> none  [the longest x12 16 us: swapped(): lax.ppermute(value, axis, [(i, i ^ 1 << bit) for i in range(lax.axis_size...]
    add x46 -> x0, other arithmetic: 20 us -> none  [the longest x6 8.41 us: local(): new_pieces.append(target_part + SOFT_RATE * (online_part - target_part))]
  transfers between devices with their start and end apart: 21 -> 0, of which waited for: 9 -> 0; matrix products, arithmetic and copies ran while one was open for 9% -> 0% of each run, Pallas kernels for 0% -> 0%
where the time goes in v1:
time: 139 us; the launch traced here: 138 us
  Pallas kernels  116 us (83%)
  local copies, waits for them, and re-layouts  17.5 us (13%)
  between operations  2.75 us (2%)
  other arithmetic  1.95 us (1%)
    pallas_call x1, Pallas kernels, local(): pl.pallas_call(functools.partial(layer_kernel, names, data_count, inside)...  116 us
    unnamed x40, local copies, waits for them, and re-layouts  6.5 us
    slice x2, local copies, waits for them, and re-layouts, unpad(): return values[:, :L].reshape((row_count,) + values.shape[2:])  3.66 us

profile of v1, /device:TPU:0, one launch (start us, length us, event | category | flops | bytes accessed | tf_op | source)
XLA Modules:
  0.0 138.5 jit_solution(3376127840795759908)
XLA Ops:
  0.6 0.0 copy-start.10
  0.7 2.5 %pad.30.refs_0_ = bf16[4,304,512]{2,1,0:T(8,128)(2,1)} pad(bf16[4,296,512]{2,1,0:T(8,128)(2,1)} %bitcast.24, bf16[]{:T(256)} %constant.21.clone.1), padding=0_0x0_8x0_0 | pad | bytes 2457602 | tf_op jit(solution)/shard_map/jit(_pad)/pad | solution.py:709
  3.2 0.0 copy-done.10
  3.2 0.1 reshape.63
  3.3 0.1 reshape.64
  3.4 0.1 reshape.65
  3.5 0.6 select_maximum_fusion.refs_7_
  4.2 0.6 pad_convert_fusion.refs_1_
  4.8 0.0 copy-done.14
  4.8 0.1 iota_compare_fusion.1
  4.8 0.6 pad_convert_fusion.4.refs_8_
  5.4 116.3 %layer.1 = (bf16[4,304,128]{2,1,0:T(8,128)(2,1)}, bf16[4,304,256]{2,1,0:T(8,128)(2,1)}, f32[8,512]{1,0:T(8,128)}, f32[8,512]{1,0:T(8,128)}, f32[8,128]{1,0:T(8,1...) custom-call(bf16[4,304,512]{2,1,0:T(8,128)(2,1)} %pad.30.refs_0_, ...), custom_call_target="tpu_custom_call" | custom-call | tf_op jit(solution)/shard_map/layer/pallas_call | solution.py:856
  121.8 1.4 %fusion = (f32[1,1]{1,0:T(1,128)}, f32[1,1]{1,0:T(1,128)}, f32[1,1]{1,0:T(1,128)}, f32[1,1]{1,0:T(1,128)}, f32[1,1]{1,0:T(1,128)}) fusion(f32[8,128]{1,0:T(8,128)} %get-tuple-element.44), kind=kLoop, calls=%fused_computation.11 | loop fusion | bytes 40 | tf_op jit(solution)/shard_map/slice | solution.py:890
  125.2 1.9 %stack.31 = f32[5]{0:T(128)} concatenate(f32[1]{0:T(128)} %bitcast.13, f32[1]{0:T(128)} %bitcast.14, f32[1]{0:T(128)} %bitcast.15, f32[1]{0:T(128)} %bitcast.16, f32[1]{0:T(128)} %bitcast.17), dimensions={0} | concatenate | bytes 40 | tf_op jit(solution)/shard_map/stack | solution.py:884
  127.1 1.3 dynamic-slice_bitcast_fusion
  128.4 2.0 %slice.22 = bf16[4,296,256]{2,1,0:T(8,128)(2,1)} slice(bf16[4,304,256]{2,1,0:T(8,128)(2,1)} %get-tuple-element.31), slice={[0:4], [0:296], [0:256]} | slice | bytes 1212416 | tf_op jit(solution)/shard_map/slice | solution.py:872
  130.3 1.7 %slice.21 = bf16[4,296,128]{2,1,0:T(8,128)(2,1)} slice(bf16[4,304,128]{2,1,0:T(8,128)(2,1)} %get-tuple-element.30), slice={[0:4], [0:296], [0:128]} | slice | bytes 606208 | tf_op jit(solution)/shard_map/slice | solution.py:872
  132.0 0.8 copy.26
  132.8 0.6 copy.36
  133.4 0.0 copy-done.7
  133.4 0.6 copy.37
  134.0 0.7 copy.38
  134.7 0.6 copy.39
  135.3 0.0 copy-done.4
  135.3 0.6 copy.40
  135.9 0.0 copy-done.6
  136.0 0.6 copy.41
  136.6 0.7 copy.42
  137.2 0.0 copy-done
  137.2 0.7 copy.43
  137.9 0.0 copy-done.8
  137.9 0.6 copy.44
  (28 shorter events, 0.1 us)
Async XLA Ops:
  0.6 2.5 %copy-start.10 = (s32[1184]{0:T(1024)S(1)}, s32[1184]{0:T(1024)}, u32[]{:S(2)}) copy-start(s32[1184]{0:T(1024)} %param.19) | copy-start | bytes 14212
  0.7 2.6 %copy-start.11 = (s32[1184]{0:T(1024)S(1)}, s32[1184]{0:T(1024)}, u32[]{:S(2)}) copy-start(s32[1184]{0:T(1024)} %param.20) | copy-start | bytes 14212
  0.7 2.7 %copy-start.12 = (s32[1184]{0:T(1024)S(1)}, s32[1184]{0:T(1024)}, u32[]{:S(2)}) copy-start(s32[1184]{0:T(1024)} %param.21) | copy-start | bytes 14212
  0.7 3.5 %copy-start.13 = (bf16[1,512,2]{1,2,0:T(2,128)(2,1)S(1)}, bf16[1,512,2]{1,2,0:T(2,128)(2,1)}, u32[]{:S(2)}) copy-start(bf16[1,512,2]{1,2,0:T(2,128)(2,1)} %param.12) | copy-start | bytes 6148
  0.7 4.1 %copy-start.14 = (s32[4]{0:T(128)S(1)}, s32[4]{0:T(128)}, u32[]{:S(2)}) copy-start(s32[4]{0:T(128)} %param.18) | copy-start | bytes 52
  121.7 10.3 %copy-start.3 = (f32[256,128]{1,0:T(8,128)S(1)}, f32[256,128]{1,0:T(8,128)}, u32[]{:S(2)}) copy-start(f32[256,128]{1,0:T(8,128)} %get-tuple-element.36) | copy-start | bytes 393220
  121.7 11.0 %copy-start.5 = (f32[32,768]{1,0:T(8,128)S(1)}, f32[32,768]{1,0:T(8,128)}, u32[]{:S(2)}) copy-start(f32[32,768]{1,0:T(8,128)} %get-tuple-element.85) | copy-start | bytes 294916
  121.8 11.7 %copy-start.7 = (f32[32,256]{1,0:T(8,128)S(1)}, f32[32,256]{1,0:T(8,128)}, u32[]{:S(2)}) copy-start(f32[32,256]{1,0:T(8,128)} %get-tuple-element.86) | copy-start | bytes 98308
  121.8 12.3 %copy-start.2 = (f32[32,1024]{1,0:T(8,128)S(1)}, f32[32,1024]{1,0:T(8,128)}, u32[]{:S(2)}) copy-start(f32[32,1024]{1,0:T(8,128)} %get-tuple-element.87) | copy-start | bytes 393220
  121.8 12.9 %copy-start.9 = (f32[32,128]{1,0:T(8,128)S(1)}, f32[32,128]{1,0:T(8,128)}, u32[]{:S(2)}) copy-start(f32[32,128]{1,0:T(8,128)} %get-tuple-element.89) | copy-start | bytes 49156
  121.8 13.5 %copy-start.4 = (f32[32,768]{1,0:T(8,128)S(1)}, f32[32,768]{1,0:T(8,128)}, u32[]{:S(2)}) copy-start(f32[32,768]{1,0:T(8,128)} %get-tuple-element.91) | copy-start | bytes 294916
  121.8 14.2 %copy-start.6 = (f32[32,256]{1,0:T(8,128)S(1)}, f32[32,256]{1,0:T(8,128)}, u32[]{:S(2)}) copy-start(f32[32,256]{1,0:T(8,128)} %get-tuple-element.92) | copy-start | bytes 98308
  121.8 14.8 %copy-start.1 = (f32[32,1024]{1,0:T(8,128)S(1)}, f32[32,1024]{1,0:T(8,128)}, u32[]{:S(2)}) copy-start(f32[32,1024]{1,0:T(8,128)} %get-tuple-element.93) | copy-start | bytes 393220
  128.3 8.9 %copy-start = (f32[128,256]{1,0:T(8,128)S(1)}, f32[128,256]{1,0:T(8,128)}, u32[]{:S(2)}) copy-start(f32[128,256]{1,0:T(8,128)} %get-tuple-element.94) | copy-start | bytes 393220
  128.4 9.5 %copy-start.8 = (f32[32,128]{1,0:T(8,128)S(1)}, f32[32,128]{1,0:T(8,128)}, u32[]{:S(2)}) copy-start(f32[32,128]{1,0:T(8,128)} %get-tuple-element.95) | copy-start | bytes 49156

commit v2 on v1

--- a/solution.py
+++ b/solution.py
@@ -65,8 +65,93 @@
     return value.reshape(value.shape[0] * value.shape[1], width)
 
 
+def without_pad(ref, s, width):
+    rows = [ref[s + i, :, :width].astype(F32)[:L] for i in range(2)]
+    return jnp.concatenate(rows, axis=0).astype(BF16)
+
+
 class Names:
     pass
+
+
+def in_steps(count, first, second, third):
+    for item in range(count + 2):
+        if item < count:
+            first(item)
+        if 0 <= item - 1 < count:
+            second(item - 1)
+        if item >= 2:
+            third(item - 2)
+
+
+def attend(n, s, d):
+    corner = lax.broadcasted_iota(jnp.int32, (128, 128), 0) >= lax.broadcasted_iota(
+        jnp.int32, (128, 128), 1
+    )
+    ones = jnp.ones((LP, 128), BF16)
+    marks = lane_halves(ones)
+    raw, raised = {}, {}
+
+    def score(pair):
+        at = 128 * pair
+        queries = lane_halves(n.qkv[s, :, at : at + 128] * jnp.array(SCORE_SCALE, BF16))
+        keys = n.qkv[s, :, d + at : d + at + 128]
+        for block, (first, rows, seen) in enumerate(BLOCKS):
+            both = jnp.concatenate([q[first : first + rows] for q in queries], axis=0)
+            raw[pair, block] = dot_nt(both, keys[:seen])
+
+    def raise_scores(pair):
+        for block, (first, rows, seen) in enumerate(BLOCKS):
+            scores = raw.pop((pair, block))
+            visible = jnp.concatenate([corner[:rows, :rows]] * 2, axis=0)
+            diagonal = jnp.where(visible, scores[:, first:], NEG_LARGE)
+            scores = jnp.concatenate([scores[:, :first], diagonal], axis=1) if first else diagonal
+            powers = jnp.exp(scores - jnp.max(scores, axis=-1, keepdims=True)).astype(BF16)
+            raised[pair, block] = powers
+            n.powers[block][s, pair] = powers
+
+    def mix(pair):
+        at = 128 * pair
+        values = lane_halves(n.qkv[s, :, 2 * d + at : 2 * d + at + 128])
+        wide = [jnp.concatenate(both, axis=1) for both in zip(values, marks)]
+        for block, (first, rows, seen) in enumerate(BLOCKS):
+            powers = raised.pop((pair, block))
+            if seen % 128 == 0:
+                mixed = dot_nn(
+                    jnp.concatenate([powers[:rows], powers[rows:]], axis=1),
+                    jnp.concatenate([w[:seen] for w in wide], axis=0),
+                )
+            else:
+                mixed = dot_nn(powers[:rows], wide[0][:seen]) + dot_nn(powers[rows:], wide[1][:seen])
+            inverse = 1.0 / mixed[:, 128:]
+            n.inverse_totals[s, first : first + rows, at : at + 128] = inverse
+            n.attended[s, first : first + rows, at : at + 128] = (mixed[:, :128] * inverse).astype(
+                BF16
+            )
+
+    in_steps(d // 128, score, raise_scores, mix)
+
+
+def lay_out_inputs(n, seq_count):
+    d = n.x.shape[2]
+    pad = jnp.zeros((LP - L, d), F32)
+    for s in range(0, seq_count, 2):
+        both = n.states[s * L : (s + 2) * L].astype(F32)
+        for i in range(2):
+            n.x[s + i] = jnp.concatenate([both[i * L : (i + 1) * L], pad], axis=0).astype(BF16)
+    n.flat[...] = jnp.zeros_like(n.flat)
+    for i, ref in enumerate((n.chosen, n.reward, n.finished)):
+        n.flat[i : i + 1, : seq_count * L] = ref[...].reshape(1, seq_count * L).astype(F32)
+    for s in range(seq_count):
+        n.aux[s] = n.flat[:, s * L : s * L + LP]
+    n.gains[...] = jnp.zeros_like(n.gains)
+    n.gains[0:2, :] = n.norm_gains[...].astype(F32)
+    seq = lax.broadcasted_iota(jnp.int32, (8, 128), 0)
+    task = lax.broadcasted_iota(jnp.int32, (8, 128), 1)
+    table = jnp.zeros((8, 128), F32)
+    for s in range(seq_count):
+        table = jnp.where(jnp.logical_and(seq == s, task == n.task_ids[s]), 1.0, table)
+    n.table[...] = table
 
 
 def forward_sequence(n, s, d):
@@ -77,28 +162,7 @@
         n.qkv[s, :, first : first + 256] = dot_nn(
             normed, n.w_qkv[:, first : first + 256]
         ).astype(BF16)
-    corner = lax.broadcasted_iota(jnp.int32, (128, 128), 0) >= lax.broadcasted_iota(
-        jnp.int32, (128, 128), 1
-    )
-    for pair in range(d // 128):
-        at = 128 * pair
-        queries = lane_halves(n.qkv[s, :, at : at + 128] * jnp.array(SCORE_SCALE, BF16))
-        keys = n.qkv[s, :, d + at : d + at + 128]
-        values = lane_halves(n.qkv[s, :, 2 * d + at : 2 * d + at + 128])
-        for block, (first, rows, seen) in enumerate(BLOCKS):
-            mixed = None
-            for head in range(2):
-                raw = dot_nt(queries[head][first : first + rows], keys[:seen])
-                diagonal = jnp.where(corner[:rows, :rows], raw[:, first:], NEG_LARGE)
-                scores = jnp.concatenate([raw[:, :first], diagonal], axis=1) if first else diagonal
-                largest = jnp.max(scores, axis=-1, keepdims=True)
-                raised = jnp.exp(scores - largest)
-                totals = jnp.sum(raised, axis=-1, keepdims=True)
-                probs = (raised * (1.0 / totals)).astype(BF16)
-                n.probs[block][s, 2 * pair + head] = probs
-                part = dot_nn(probs, values[head][:seen])
-                mixed = part if mixed is None else mixed + part
-            n.attended[s, first : first + rows, at : at + 128] = mixed.astype(BF16)
+    attend(n, s, d)
     middle = x + dot_nn(n.attended[s], n.w_out[...])
     n.middle[s] = middle
     normed = (middle * inverse_rms(middle) * n.gains[1:2, :]).astype(BF16)
@@ -149,42 +213,69 @@
     n.grad_mixed[s] = dot_nt(grad_branch, n.w_out[...]).astype(BF16)
 
 
-def backward_attention(n, s, d):
-    lane = lax.broadcasted_iota(jnp.int32, (1, 128), 1)
-    for pair in range(d // 128):
+def attend_back(n, s, d):
+    side = lax.broadcasted_iota(jnp.int32, (256, 256), 0) % 128 < HEAD_DIM
+    head = lax.broadcasted_iota(jnp.int32, (256, 256), 1) < 128
+    head_sums = jnp.where(side == head, jnp.ones((), BF16), jnp.zeros((), BF16))
+    kept = {}
+
+    def spread(pair):
         at = 128 * pair
+        grads = (
+            n.grad_mixed[s, :, at : at + 128].astype(F32) * n.inverse_totals[s, :, at : at + 128]
+        ).astype(BF16)
+        product = n.attended[s, :, at : at + 128].astype(F32) * grads.astype(F32)
+        upper = product.astype(BF16)
+        lower = (product - upper.astype(F32)).astype(BF16)
+        centres = dot_nn(jnp.concatenate([upper, lower], axis=1), head_sums)
         values = n.qkv[s, :, 2 * d + at : 2 * d + at + 128]
-        grad_mixed = n.grad_mixed[s, :, at : at + 128]
-        product = n.attended[s, :, at : at + 128].astype(F32) * grad_mixed.astype(F32)
-        centres = (
-            jnp.sum(jnp.where(lane < HEAD_DIM, product, 0.0), axis=-1, keepdims=True),
-            jnp.sum(jnp.where(lane >= HEAD_DIM, product, 0.0), axis=-1, keepdims=True),
-        )
+        grads = lane_halves(grads)
+        found = []
+        for first, rows, seen in BLOCKS:
+            both = jnp.concatenate([g[first : first + rows] for g in grads], axis=0)
+            found.append((both, dot_nt(both, values[:seen])))
+        kept[pair] = centres, found
+
+    def centre(pair):
+        centres, found = kept[pair]
+        done = []
+        for block, (first, rows, seen) in enumerate(BLOCKS):
+            both, grad_powers = found[block]
+            here = centres[first : first + rows]
+            here = jnp.concatenate([here[:, :128], here[:, 128:]], axis=0)
+            here = jnp.concatenate([here] * ((seen + 127) // 128), axis=1)[:, :seen]
+            powers = n.powers[block][s, pair]
+            done.append((both, powers, (powers.astype(F32) * (grad_powers - here)).astype(BF16)))
+        kept[pair] = done
+
+    def collect(pair):
+        at = 128 * pair
         queries = lane_halves(n.qkv[s, :, at : at + 128])
         keys = lane_halves(n.qkv[s, :, d + at : d + at + 128])
-        grads = lane_halves(grad_mixed)
         grad_keys = [None] * 3
         grad_values = [None] * 3
+        done = kept.pop(pair)
         for block, (first, rows, seen) in enumerate(BLOCKS):
-            grad_queries = None
-            for head in range(2):
-                probs = n.probs[block][s, 2 * pair + head]
-                here = grads[head][first : first + rows]
-                grad_probs = dot_nt(here, values[:seen])
-                grad_scores = (
-                    probs.astype(F32) * (grad_probs - centres[head][first : first + rows])
-                ).astype(BF16)
-                part = dot_nn(grad_scores, keys[head][:seen])
-                grad_queries = part if grad_queries is None else grad_queries + part
-                of_values = dot_tn(probs, here)
-                of_keys = dot_tn(grad_scores, queries[head][first : first + rows])
-                for i, start in enumerate((0, 128, 256)):
-                    if start < seen:
-                        end = min(start + 128, seen)
-                        piece = of_values[start:end]
-                        grad_values[i] = piece if grad_values[i] is None else grad_values[i] + piece
-                        piece = of_keys[start:end]
-                        grad_keys[i] = piece if grad_keys[i] is None else grad_keys[i] + piece
+            both, powers, grad_scores = done[block]
+            both_queries = jnp.concatenate([q[first : first + rows] for q in queries], axis=0)
+            if seen % 128 == 0:
+                grad_queries = dot_nn(
+                    jnp.concatenate([grad_scores[:rows], grad_scores[rows:]], axis=1),
+                    jnp.concatenate([k[:seen] for k in keys], axis=0),
+                )
+            else:
+                grad_queries = dot_nn(grad_scores[:rows], keys[0][:seen]) + dot_nn(
+                    grad_scores[rows:], keys[1][:seen]
+                )
+            of_values = dot_tn(powers, both)
+            of_keys = dot_tn(grad_scores, both_queries)
+            for i, start in enumerate((0, 128, 256)):
+                if start < seen:
+                    end = min(start + 128, seen)
+                    piece = of_values[start:end]
+                    grad_values[i] = piece if grad_values[i] is None else grad_values[i] + piece
+                    piece = of_keys[start:end]
+                    grad_keys[i] = piece if grad_keys[i] is None else grad_keys[i] + piece
             n.qkv[s, first : first + rows, at : at + 128] = (grad_queries * SCORE_SCALE).astype(
                 BF16
             )
@@ -195,6 +286,12 @@
             n.qkv[s, first : first + rows, 2 * d + at : 2 * d + at + 128] = grad_values[i].astype(
                 BF16
             )
+
+    in_steps(d // 128, spread, centre, collect)
+
+
+def backward_attention(n, s, d):
+    attend_back(n, s, d)
     grad_one = dot_nt(n.qkv[s], n.w_qkv[...])
     x = n.x[s].astype(F32)
     inverse = inverse_rms(x)
@@ -215,7 +312,7 @@
     n = Names()
     for name, ref in zip(names, refs):
         setattr(n, name, ref)
-    n.probs = (n.probs_0, n.probs_1, n.probs_2)
+    n.powers = (n.powers_0, n.powers_1, n.powers_2)
     d = n.x.shape[2]
     ff = n.w_up.shape[1]
     seq_count = n.x.shape[0]
@@ -311,6 +408,7 @@
         )
 
     n.gain_sums[...] = jnp.zeros_like(n.gain_sums)
+    lay_out_inputs(n, seq_count)
 
     @pl.loop(0, seq_count)
     def _(s):
@@ -647,9 +745,9 @@
                 gain_copy(2, k).start()
         owner_online("up")
         axis_done("qkv")
-        for s in range(seq_count):
-            n.state_out[s] = n.grad_states[s, :, : d // 2]
-        n.q_out[...] = n.q_rows[:, :, :128]
+        for s in range(0, seq_count, 2):
+            n.state_out[s * L : (s + 2) * L] = without_pad(n.grad_states, s, d // 2)
+            n.q_out[s * L : (s + 2) * L] = without_pad(n.q_rows, s, 128)
         owner_online("out")
         owner_online("head")
         if inside:
@@ -676,12 +774,14 @@
         stat_second()
         stat_third()
         q_copy().wait_recv()
-        n.q_out[...] = n.q_half[...]
+        for s in range(0, seq_count, 2):
+            n.q_out[s * L : (s + 2) * L] = without_pad(n.q_half, s, 128)
         for name in TENSORS[:4]:
             owner_target(name)
         for s in range(seq_count):
             state_copy(s).wait_recv()
-            n.state_out[s] = n.state_half[s]
+            if s % 2:
+                n.state_out[(s - 1) * L : (s + 1) * L] = without_pad(n.state_half, s - 1, d // 2)
         if inside:
             total = None
             for k in range(3, 7):
@@ -704,9 +804,54 @@
     assert used[0] <= SEMAPHORES
 
 
-def pad_rows(values, seq_count):
-    shaped = values.reshape((seq_count, L) + values.shape[1:])
-    return jnp.pad(shaped, ((0, 0), (0, LP - L)) + ((0, 0),) * (shaped.ndim - 2))
+OUTPUTS = (
+    "q_out",
+    "state_out",
+    "grad_gains",
+    "grad_qkv",
+    "grad_out",
+    "grad_up",
+    "grad_down",
+    "grad_head",
+    "new_gains",
+    "new_qkv",
+    "new_out",
+    "new_up",
+    "new_down",
+    "new_head",
+    "stats",
+)
+
+
+def finish_kernel(moved, worked, token_total, data_count, *refs):
+    source = dict(zip(moved + worked, refs))
+    result = dict(zip(OUTPUTS, refs[len(source) :]))
+    sems = refs[-1]
+    copies = [
+        pltpu.make_async_copy(source[name], result[name], sems.at[i])
+        for i, name in enumerate(moved)
+    ]
+    for copy in copies:
+        copy.start()
+    me_pair = lax.axis_index("pair")
+    me = lax.axis_index("dp")
+    for name in ("grad_gains", "new_gains"):
+        height = source[name].shape[1] // data_count
+        here = source[name][:, pl.ds(pl.multiple_of(me * height // 128 * 128, 128), 128)]
+        value = here[:, :height]
+        for at in range(height, 128, height):
+            value = jnp.where(me * height % 128 == at, here[:, at : at + height], value)
+        result[name][...] = jnp.where(me_pair == 0, value[0:1], value[1:2])
+    if "grad_down" in worked:
+        result["grad_down"][...] = jnp.transpose(source["grad_down"][...])
+    stats = source["stats"]
+    result["stats"][0] = stats[0, 0] / token_total
+    result["stats"][1] = stats[0, 1] / token_total
+    result["stats"][2] = stats[1, 0]
+    result["stats"][3] = stats[0, 2] / token_total
+    result["stats"][4] = stats[1, 1]
+    for copy in copies:
+        copy.wait()
 
 
 def add_outside(out, params, pair_index, data_index, data_count):
@@ -761,28 +906,23 @@
     bin_count = w_head.shape[2]
     seq_count = row_count // L
 
-    x = pad_rows(states[0], seq_count)
-    gains = jnp.pad(norm_gains[0].astype(F32).T, ((0, 6), (0, 0)))
-    aux = jnp.stack([pad_rows(a, seq_count).astype(F32) for a in (chosen, reward, finished)], axis=1)
-    aux = jnp.pad(aux, ((0, 0), (0, 5), (0, 0)))
-    table = (task_ids[:, None] == jnp.arange(128, dtype=jnp.int32)[None, :]).astype(F32)
-    table = jnp.pad(table, ((0, 8 - seq_count), (0, 0)))
-
     inside = data_count == 16
-    heads = d // HEAD_DIM
     rows = (seq_count, LP, d)
     inputs = dict(
-        x=x,
-        gains=gains,
+        states=states[0],
+        norm_gains=norm_gains[0].T,
         w_qkv=w_qkv[0],
         w_out=w_out[0],
         w_up=w_up[0],
         w_down=w_down[0],
         w_head=w_head[0],
-        aux=aux,
-        table=table,
+        task_ids=task_ids,
+        chosen=chosen,
+        reward=reward,
+        finished=finished,
     )
     if not inside:
+        table = (task_ids[:, None] == jnp.arange(128, dtype=jnp.int32)[None, :]).astype(F32)
         inputs["counts"] = jnp.broadcast_to(
             lax.psum(jnp.sum(table, axis=0, keepdims=True), "dp"), (8, 128)
         )
@@ -799,8 +939,8 @@
     }
     new_shapes = dict(halves, down=(ff // 16, d // 2))
     outputs = dict(
-        q_out=((seq_count, LP, bin_count // 2), BF16),
-        state_out=((seq_count, LP, d // 2), BF16),
+        q_out=((row_count, bin_count // 2), BF16),
+        state_out=((row_count, d // 2), BF16),
         grad_gains=((8, d), F32),
         new_gains=((8, d), F32),
         stats=((8, 128), F32),
@@ -812,11 +952,17 @@
         else:
             outputs["g_" + name] = ((2, 2, 2, 2) + piece[name], BF16)
     scratch = dict(
+        x=(rows, BF16),
+        gains=((8, d), F32),
+        flat=((8, -(-(row_count + LP - L) // 128) * 128), F32),
+        aux=((seq_count, 8, LP), F32),
+        table=((8, 128), F32),
         normed_one=(rows, BF16),
         qkv=((seq_count, LP, 3 * d), BF16),
-        probs_0=((seq_count, heads) + (BLOCKS[0][1], BLOCKS[0][2]), BF16),
-        probs_1=((seq_count, heads) + (BLOCKS[1][1], BLOCKS[1][2]), BF16),
-        probs_2=((seq_count, heads) + (BLOCKS[2][1], BLOCKS[2][2]), BF16),
+        powers_0=((seq_count, d // 128) + (2 * BLOCKS[0][1], BLOCKS[0][2]), BF16),
+        powers_1=((seq_count, d // 128) + (2 * BLOCKS[1][1], BLOCKS[1][2]), BF16),
+        powers_2=((seq_count, d // 128) + (2 * BLOCKS[2][1], BLOCKS[2][2]), BF16),
+        inverse_totals=(rows, F32),
         attended=(rows, BF16),
         middle=(rows, F32),
         normed_two=(rows, BF16),
@@ -853,10 +999,11 @@
         scratch["their_" + name] = (new_shapes[name], BF16)
     names = list(inputs) + list(outputs) + list(scratch) + ["send_sem", "recv_sem"]
     in_vmem = pl.BlockSpec(memory_space=pltpu.VMEM)
+    in_smem = pl.BlockSpec(memory_space=pltpu.SMEM)
     raw = pl.pallas_call(
         functools.partial(layer_kernel, names, data_count, inside),
         out_shape=[jax.ShapeDtypeStruct(shape, dtype) for shape, dtype in outputs.values()],
-        in_specs=[in_vmem] * len(inputs),
+        in_specs=[in_smem if name == "task_ids" else in_vmem for name in inputs],
         out_specs=[in_vmem] * len(outputs),
         scratch_shapes=[pltpu.VMEM(shape, dtype) for shape, dtype in scratch.values()]
         + [pltpu.SemaphoreType.DMA((SEMAPHORES,)), pltpu.SemaphoreType.DMA((SEMAPHORES,))],
@@ -866,47 +1013,36 @@
         name="layer",
     )(*inputs.values())
     out = dict(zip(outputs, raw))
-    token_total = row_count * data_count
-
-    def unpad(values):
-        return values[:, :L].reshape((row_count,) + values.shape[2:])
-
     if not inside:
         params = (norm_gains[0], w_qkv[0], w_out[0], w_up[0], w_down[0], w_head[0])
         add_outside(out, params, pair_index, data_index, data_count)
-    height = d // data_count
-
-    def gains_piece(values):
-        return lax.dynamic_slice(values, (pair_index, data_index * height), (1, height)).reshape(
-            height, 1
-        )
-
-    stats = jnp.stack(
-        [
-            out["stats"][0, 0] / token_total,
-            out["stats"][0, 1] / token_total,
-            out["stats"][1, 0],
-            out["stats"][0, 2] / token_total,
-            out["stats"][1, 1],
-        ]
-    )
-    return (
-        unpad(out["q_out"]),
-        unpad(out["state_out"]),
-        gains_piece(out["grad_gains"]),
-        out["grad_qkv"],
-        out["grad_out"],
-        out["grad_up"],
-        out["grad_down"].T if inside else out["grad_down"],
-        out["grad_head"],
-        gains_piece(out["new_gains"]),
-        out["new_qkv"],
-        out["new_out"],
-        out["new_up"],
-        out["new_down"],
-        out["new_head"],
-        stats,
-    )
+    moved = {name: out[name] for name in OUTPUTS if name not in ("grad_gains", "new_gains", "stats")}
+    worked = {name: out[name] for name in ("grad_gains", "new_gains", "stats")}
+    results = {name: jax.ShapeDtypeStruct(value.shape, value.dtype) for name, value in moved.items()}
+    if inside:
+        worked["grad_down"] = moved.pop("grad_down")
+        results["grad_down"] = jax.ShapeDtypeStruct((ff // data_count, d // 2), F32)
+    results["grad_gains"] = results["new_gains"] = jax.ShapeDtypeStruct((1, d // data_count), F32)
+    results["stats"] = jax.ShapeDtypeStruct((5,), F32)
+    anywhere = pl.BlockSpec(memory_space=pl.ANY)
+    spec_of = {name: anywhere if name in moved else in_vmem for name in OUTPUTS}
+    spec_of["stats"] = in_smem
+    final = pl.pallas_call(
+        functools.partial(
+            finish_kernel, list(moved), list(worked), row_count * data_count, data_count
+        ),
+        out_shape=[results[name] for name in OUTPUTS],
+        in_specs=[in_vmem] * (len(moved) + len(worked)),
+        out_specs=[spec_of[name] for name in OUTPUTS],
+        scratch_shapes=[
+            pltpu.SemaphoreType.DMA((len(moved),)),
+        ],
+        name="finish",
+    )(*moved.values(), *worked.values())
+    final = dict(zip(OUTPUTS, final))
+    for name in ("grad_gains", "new_gains"):
+        final[name] = final[name].T
+    return tuple(final.values())
 
 
 def solution(mesh):

time: 139 us -> 104 us (0.75)
  local copies, waits for them, and re-layouts: 17.5 us -> 0 us
  Pallas kernels: 116 us -> 103 us
  other arithmetic: 1.95 us -> 0 us
  between operations: 2.75 us -> 0.82 us
    pallas_call x1, Pallas kernels: 116 us -> 99.7 us  [local(): pl.pallas_call(functools.partial(layer_kernel, names, data_count, inside)...]
    unnamed x40 -> x0, local copies, waits for them, and re-layouts: 6.5 us -> none
    slice x3 -> x0, local copies, waits for them, and re-layouts: 5.09 us -> none  [the longest x2 3.66 us: unpad(): return values[:, :L].reshape((row_count,) + values.shape[2:])]
    pallas_call x0 -> x1, Pallas kernels: none -> 3.38 us  [local(): pl.pallas_call(functools.partial(finish_kernel, list(moved), list(worked)...]
    pad x1 -> x0, local copies, waits for them, and re-layouts: 2.49 us -> none  [pad_rows(): jnp.pad(shaped, ((0, 0), (0, LP - L)) + ((0, 0),) * (shaped.ndim - 2))]
    another operation x4 -> x0, local copies, waits for them, and re-layouts: 1.91 us -> none  [the longest x1 1.89 us: local(): jnp.stack([out['stats'][0, 0] / token_total, out['stats'][0, 1] / token_t...]
    reshape x4 -> x0, local copies, waits for them, and re-layouts: 1.5 us -> none  [the longest x1 1.26 us: gains_piece(): lax.dynamic_slice(values, (pair_index, data_index * height), (1, height))]
where the time goes in v2:
time: 104 us
  Pallas kernels  103 us (99%)
    pallas_call x1, Pallas kernels, local(): pl.pallas_call(functools.partial(layer_kernel, names, data_count, inside)...  99.7 us
    pallas_call x1, Pallas kernels, local(): pl.pallas_call(functools.partial(finish_kernel, list(moved), list(worked)...  3.38 us

profile of v2, /device:TPU:0, one launch (start us, length us, event | category | flops | bytes accessed | tf_op | source)
XLA Modules:
  0.0 103.9 jit_solution(5607254887698613932)
XLA Ops:
  0.6 99.7 %layer.1 = (bf16[1184,128]{1,0:T(8,128)(2,1)}, bf16[1184,256]{1,0:T(8,128)(2,1)}, f32[8,512]{1,0:T(8,128)}, f32[8,512]{1,0:T(8,128)}, f32[8,128]{1,0:T(8,128)}, ...) custom-call(bf16[1184,512]{1,0:T(8,128)(2,1)} %bitcast.14, ...), custom_call_target="tpu_custom_call" | custom-call | tf_op jit(solution)/shard_map/layer/pallas_call | solution.py:1003
  100.3 3.4 %finish.1 = (bf16[1184,128]{1,0:T(8,128)(2,1)}, bf16[1184,256]{1,0:T(8,128)(2,1)}, f32[1,32]{1,0:T(1,128)}, f32[32,768]{1,0:T(8,128)}, f32[32,256]{1,0:T(8,128)}...) custom-call(bf16[1184,128]{1,0:T(8,128)(2,1)} %get-tuple-element.45., ...), custom_call_target="tpu_custom_call" | custom-call | tf_op jit(solution)/shard_map/finish/pallas_call | solution.py:1030

commit v3 on v2

v3 whole, which is shorter than its diff:
```python
import functools

import jax
import jax.numpy as jnp
from jax import lax
from jax.experimental import pallas as pl
from jax.experimental.pallas import tpu as pltpu
from jax.sharding import PartitionSpec as P

F32 = jnp.float32
BF16 = jnp.bfloat16
MESH = pl.DeviceIdType.MESH

DOWN = "down"
PAIR = "pair"
DP = "dp"
STATS = "stats"
ROW = "row"
HEAD = "head"
UP_B = "up_b"
OUT = "out"
UP_A = "up_a"
LOW = "low"
GRAD_GAINS = "grad_gains"
HIGH = "high"
GRAD_DOWN = "grad_down"
NEW_GAINS = "new_gains"
QKV_0 = "qkv_0"
QKV_1 = "qkv_1"
QKV_2 = "qkv_2"
QKV_3 = "qkv_3"
UP = "up"
QKV = "qkv"
GAINS = "gains"

HEAD_DIM = 64
L = 296
LP = 304
TASKS = 32
EPSILON = 1e-06
DISCOUNT = 0.98
SOFT_RATE = 0.2
SCORE_SCALE = 0.125
NEG_LARGE = -1000000000.0
LOWEST = -1e30

BLOCKS = ((0, 128, 128), (128, 128, 256), (256, 48, 304))


def dot_nn(a, b):
    return lax.dot_general(a, b, (((1,), (0,)), ((), ())), preferred_element_type=F32)


def dot_nt(a, b):
    return lax.dot_general(a, b, (((1,), (1,)), ((), ())), preferred_element_type=F32)


def dot_tn(a, b):
    return lax.dot_general(a, b, (((0,), (0,)), ((), ())), preferred_element_type=F32)


def dot_tt(a, b):
    return lax.dot_general(a, b, (((0,), (1,)), ((), ())), preferred_element_type=F32)


def inverse_rms(values):
    return lax.rsqrt(jnp.mean(values * values, axis=-1, keepdims=True) + EPSILON)


def gelu_and_slope(u):
    c = 0.7978845608028654
    square = u * u
    t = jnp.tanh(u * (c + (c * 0.044715) * square))
    half = 0.5 * t + 0.5
    slope = half + (u * (0.5 - 0.5 * t * t)) * (c + (3 * c * 0.044715) * square)
    return u * half, slope


def lane_halves(a):
    lane = lax.broadcasted_iota(jnp.int32, (1, 2 * HEAD_DIM), 1)
    zero = jnp.zeros((), a.dtype)
    return jnp.where(lane < HEAD_DIM, a, zero), jnp.where(lane >= HEAD_DIM, a, zero)


def rows_of(ref, first, width):
    value = ref[:, :, first : first + width]
    return value.reshape(value.shape[0] * value.shape[1], width)


def without_pad(ref, s, width):
    rows = [ref[s + i, :, :width].astype(F32)[:L] for i in range(2)]
    return jnp.concatenate(rows, axis=0).astype(BF16)


class Names:
    pass


def in_steps(count, first, second, third):
    for item in range(count + 2):
        if item < count:
            first(item)
        if 0 <= item - 1 < count:
            second(item - 1)
        if item >= 2:
            third(item - 2)


def attend(n, items, d):
    corner = lax.broadcasted_iota(jnp.int32, (128, 128), 0) >= lax.broadcasted_iota(
        jnp.int32, (128, 128), 1
    )
    ones = jnp.ones((LP, 128), BF16)
    marks = lane_halves(ones)
    raw, raised = {}, {}

    def score(item):
        s, pair = items[item]
        at = 128 * pair
        queries = lane_halves(n.qkv[s, :, at : at + 128] * jnp.array(SCORE_SCALE, BF16))
        keys = n.qkv[s, :, d + at : d + at + 128]
        for block, (first, rows, seen) in enumerate(BLOCKS):
            both = jnp.concatenate([q[first : first + rows] for q in queries], axis=0)
            raw[item, block] = dot_nt(both, keys[:seen])

    def raise_scores(item):
        s, pair = items[item]
        for block, (first, rows, seen) in enumerate(BLOCKS):
            scores = raw.pop((item, block))
            visible = jnp.concatenate([corner[:rows, :rows]] * 2, axis=0)
            diagonal = jnp.where(visible, scores[:, first:], NEG_LARGE)
            scores = jnp.concatenate([scores[:, :first], diagonal], axis=1) if first else diagonal
            powers = jnp.exp(scores - jnp.max(scores, axis=-1, keepdims=True)).astype(BF16)
            raised[item, block] = powers
            n.powers[block][s, pair] = powers

    def mix(item):
        s, pair = items[item]
        at = 128 * pair
        values = lane_halves(n.qkv[s, :, 2 * d + at : 2 * d + at + 128])
        wide = [jnp.concatenate(both, axis=1) for both in zip(values, marks)]
        for block, (first, rows, seen) in enumerate(BLOCKS):
            powers = raised.pop((item, block))
            if seen % 128 == 0:
                mixed = dot_nn(
                    jnp.concatenate([powers[:rows], powers[rows:]], axis=1),
                    jnp.concatenate([w[:seen] for w in wide], axis=0),
                )
            else:
                mixed = dot_nn(powers[:rows], wide[0][:seen]) + dot_nn(powers[rows:], wide[1][:seen])
            inverse = 1.0 / mixed[:, 128:]
            n.inverse_totals[s, first : first + rows, at : at + 128] = inverse
            n.attended[s, first : first + rows, at : at + 128] = (mixed[:, :128] * inverse).astype(
                BF16
            )

    in_steps(len(items), score, raise_scores, mix)


def lay_out_inputs(n, seq_count):
    d = n.x.shape[2]
    pad = jnp.zeros((LP - L, d), F32)
    for s in range(0, seq_count, 2):
        both = n.states[s * L : (s + 2) * L].astype(F32)
        for i in range(2):
            n.x[s + i] = jnp.concatenate([both[i * L : (i + 1) * L], pad], axis=0).astype(BF16)
    n.flat[...] = jnp.zeros_like(n.flat)
    for i, ref in enumerate((n.chosen, n.reward, n.finished)):
        n.flat[i : i + 1, : seq_count * L] = ref[...].reshape(1, seq_count * L).astype(F32)
    for s in range(seq_count):
        n.aux[s] = n.flat[:, s * L : s * L + LP]
    n.gains[...] = jnp.zeros_like(n.gains)
    n.gains[0:2, :] = n.norm_gains[...].astype(F32)
    seq = lax.broadcasted_iota(jnp.int32, (8, 128), 0)
    task = lax.broadcasted_iota(jnp.int32, (8, 128), 1)
    table = jnp.zeros((8, 128), F32)
    for s in range(seq_count):
        table = jnp.where(jnp.logical_and(seq == s, task == n.task_ids[s]), 1.0, table)
    n.table[...] = table


def forward_sequences(n, s, online, loads):
    both = pl.ds(s, 2)
    d = n.x.shape[2]
    ff = n.w_up.shape[1]

    def rows(ref):
        return ref[both].reshape(2 * LP, ref.shape[2])

    def split(value):
        return value.astype(BF16).reshape(2, LP, value.shape[1])

    x = rows(n.x).astype(F32)
    normed = (x * inverse_rms(x) * n.gains[0:1, :]).astype(BF16)
    n.normed_one[both] = split(normed)
    for first in range(0, 3 * d, 256):
        n.qkv[both, :, first : first + 256] = split(
            dot_nn(normed, n.w_qkv[:, first : first + 256])
        )
    attend(n, [(s + i, pair) for i in range(2) for pair in range(d // 128)], d)

    @pl.when(s == 0)
    def _():
        for load in loads:
            load.wait()

    middle = rows(n.x).astype(F32) + dot_nn(rows(n.attended), n.w_out[...])
    n.middle[both] = middle.reshape(2, LP, d)
    normed = (middle * inverse_rms(middle) * n.gains[1:2, :]).astype(BF16)
    n.normed_two[both] = split(normed)

    @pl.when(online)
    def _():
        for first in range(0, ff, 256):
            active, slope = gelu_and_slope(dot_nn(normed, n.w_up[:, first : first + 256]))
            n.active[both, :, first : first + 256] = split(active)
            n.slope[both, :, first : first + 256] = split(slope)

    @pl.when(jnp.logical_not(online))
    def _():
        for first in range(0, ff, 256):
            active, _ = gelu_and_slope(dot_nn(normed, n.w_up[:, first : first + 256]))
            n.active[both, :, first : first + 256] = split(active)

    final_low = (rows(n.middle) + dot_nn(rows(n.active), n.w_down[...])).astype(BF16)
    n.final_low[both] = split(final_low)
    n.q_rows[both] = split(dot_nn(final_low, n.w_head[...]))
    for i in range(2):
        q_columns = dot_tt(n.w_head[...], n.final_low[s + i])
        bins = lax.broadcasted_iota(jnp.int32, q_columns.shape, 0)
        chosen = n.aux[s + i, 0:1, :].astype(jnp.int32)
        n.picked[pl.ds(s + i, 1), :] = jnp.sum(
            jnp.where(bins == chosen, q_columns, 0.0), axis=0, keepdims=True
        )
        n.tops[pl.ds(s + i, 1), :] = jnp.max(q_columns, axis=0, keepdims=True)


def backward_head(n, s):
    bins = lax.broadcasted_iota(jnp.int32, (n.w_head.shape[1], LP), 0)
    chosen = n.aux[s, 0:1, :].astype(jnp.int32)
    grad_q = jnp.where(bins == chosen, n.coef[pl.ds(s, 1), :], 0.0).astype(BF16)
    n.grad_q[s] = grad_q
    n.grad_ffn[s] = dot_tt(grad_q, n.w_head[...]).astype(BF16)


def backward_upper(n, s):
    both = pl.ds(s, 2)
    ff = n.w_up.shape[1]
    grad_ffn = n.grad_ffn[both].reshape(2 * LP, -1)
    for first in range(0, ff, 256):
        grad_active = dot_nt(grad_ffn, n.w_down[first : first + 256, :])
        slope = n.slope[both, :, first : first + 256].astype(F32)
        n.slope[both, :, first : first + 256] = (
            grad_active.reshape(2, LP, 256) * slope
        ).astype(BF16)


def backward_middle(n, s):
    both = pl.ds(s, 2)
    d = n.x.shape[2]
    grad_two = dot_nt(n.slope[both].reshape(2 * LP, -1), n.w_up[...])
    middle = n.middle[both].reshape(2 * LP, d)
    inverse = inverse_rms(middle)
    normal = middle * inverse
    n.gain_sums[1] += jnp.sum((grad_two * normal).reshape(2 * LP // 8, 8, d), axis=0)
    inner = grad_two * n.gains[1:2, :]
    grad_final = jnp.concatenate(
        [dot_tt(n.grad_q[s + i], n.w_head[...]) for i in range(2)], axis=0
    )
    grad_middle = grad_final + inverse * (
        inner - normal * jnp.mean(inner * normal, axis=-1, keepdims=True)
    )
    n.middle[both] = grad_middle.reshape(2, LP, d)
    grad_branch = grad_middle.astype(BF16)
    n.grad_branch[both] = grad_branch.reshape(2, LP, d)
    n.grad_mixed[both] = dot_nt(grad_branch, n.w_out[...]).astype(BF16).reshape(2, LP, d)


def attend_back(n, items, d):
    side = lax.broadcasted_iota(jnp.int32, (256, 256), 0) % 128 < HEAD_DIM
    head = lax.broadcasted_iota(jnp.int32, (256, 256), 1) < 128
    head_sums = jnp.where(side == head, jnp.ones((), BF16), jnp.zeros((), BF16))
    kept = {}

    def spread(item):
        s, pair = items[item]
        at = 128 * pair
        grads = (
            n.grad_mixed[s, :, at : at + 128].astype(F32) * n.inverse_totals[s, :, at : at + 128]
        ).astype(BF16)
        product = n.attended[s, :, at : at + 128].astype(F32) * grads.astype(F32)
        upper = product.astype(BF16)
        lower = (product - upper.astype(F32)).astype(BF16)
        centres = dot_nn(jnp.concatenate([upper, lower], axis=1), head_sums)
        values = n.qkv[s, :, 2 * d + at : 2 * d + at + 128]
        grads = lane_halves(grads)
        found = []
        for first, rows, seen in BLOCKS:
            both = jnp.concatenate([g[first : first + rows] for g in grads], axis=0)
            found.append((both, dot_nt(both, values[:seen])))
        kept[item] = centres, found

    def centre(item):
        s, pair = items[item]
        centres, found = kept[item]
        done = []
        for block, (first, rows, seen) in enumerate(BLOCKS):
            both, grad_powers = found[block]
            here = centres[first : first + rows]
            here = jnp.concatenate([here[:, :128], here[:, 128:]], axis=0)
            here = jnp.concatenate([here] * ((seen + 127) // 128), axis=1)[:, :seen]
            powers = n.powers[block][s, pair]
            done.append((both, powers, (powers.astype(F32) * (grad_powers - here)).astype(BF16)))
        kept[item] = done

    def collect(item):
        s, pair = items[item]
        at = 128 * pair
        queries = lane_halves(n.qkv[s, :, at : at + 128])
        keys = lane_halves(n.qkv[s, :, d + at : d + at + 128])
        grad_keys = [None] * 3
        grad_values = [None] * 3
        done = kept.pop(item)
        for block, (first, rows, seen) in enumerate(BLOCKS):
            both, powers, grad_scores = done[block]
            both_queries = jnp.concatenate([q[first : first + rows] for q in queries], axis=0)
            if seen % 128 == 0:
                grad_queries = dot_nn(
                    jnp.concatenate([grad_scores[:rows], grad_scores[rows:]], axis=1),
                    jnp.concatenate([k[:seen] for k in keys], axis=0),
                )
            else:
                grad_queries = dot_nn(grad_scores[:rows], keys[0][:seen]) + dot_nn(
                    grad_scores[rows:], keys[1][:seen]
                )
            of_values = dot_tn(powers, both)
            of_keys = dot_tn(grad_scores, both_queries)
            for i, start in enumerate((0, 128, 256)):
                if start < seen:
                    end = min(start + 128, seen)
                    piece = of_values[start:end]
                    grad_values[i] = piece if grad_values[i] is None else grad_values[i] + piece
                    piece = of_keys[start:end]
                    grad_keys[i] = piece if grad_keys[i] is None else grad_keys[i] + piece
            n.qkv[s, first : first + rows, at : at + 128] = (grad_queries * SCORE_SCALE).astype(
                BF16
            )
        for i, (first, rows, _) in enumerate(BLOCKS):
            n.qkv[s, first : first + rows, d + at : d + at + 128] = (
                grad_keys[i] * SCORE_SCALE
            ).astype(BF16)
            n.qkv[s, first : first + rows, 2 * d + at : 2 * d + at + 128] = grad_values[i].astype(
                BF16
            )

    in_steps(len(items), spread, centre, collect)


def backward_states(n, s):
    grad_one = dot_nt(n.qkv[s], n.w_qkv[...])
    x = n.x[s].astype(F32)
    inverse = inverse_rms(x)
    normal = x * inverse
    n.gain_sums[0] += jnp.sum((grad_one * normal).reshape(LP // 8, 8, -1), axis=0)
    inner = grad_one * n.gains[0:1, :]
    n.grad_states[s] = (
        n.middle[s]
        + inverse * (inner - normal * jnp.mean(inner * normal, axis=-1, keepdims=True))
    ).astype(BF16)


ROUTES = {
    DOWN: (ROW,),
    HEAD: (ROW,),
    UP_A: (ROW, LOW, HIGH),
    UP_B: (LOW, ROW, HIGH),
    OUT: (ROW,),
    QKV_0: (ROW,),
    QKV_1: (LOW,),
    QKV_2: (ROW,),
    QKV_3: (LOW,),
}
CHUNKS = {
    QKV_0: ((0, 128), (0, 128)),
    QKV_1: ((256, 384), (256, 384)),
    QKV_2: ((512,), (512,)),
    QKV_3: ((640,), (640,)),
}
STRIDES = {HIGH: 8, LOW: 4, ROW: 2}
TENSORS = (DOWN, HEAD, UP, OUT, QKV)
AXES = (HIGH, LOW, ROW)
SEMAPHORES = 128


def layer_kernel(names, data_count, inside, *refs):
    n = Names()
    for name, ref in zip(names, refs):
        setattr(n, name, ref)
    n.powers = (n.powers_0, n.powers_1, n.powers_2)
    n.grad_states, n.grad_branch, n.grad_mixed = n.normed_one, n.normed_two, n.final_low
    d = n.x.shape[2]
    ff = n.w_up.shape[1]
    seq_count = n.x.shape[0]

    me_pair = lax.axis_index(PAIR)
    me = lax.axis_index(DP)
    other = 1 - me_pair
    online = me_pair == 0
    core = me % 2
    row = (me // 2) % 2
    low = (me // 4) % 2
    high = me // 8
    quarter = me // 4
    bits = {ROW: row, LOW: low, HIGH: high}
    sibling = (me_pair, me + 1 - 2 * core)
    partner = (other, me)
    across = {
        "core": sibling,
        ROW: (me_pair, me + 2 - 4 * row),
        LOW: (me_pair, me + 4 - 8 * low),
        HIGH: (me_pair, me + 8 - 16 * high),
        PAIR: partner,
    }

    def at_quarter(which, pair):
        return (pair, me + 4 * (which - quarter))

    used = [0]

    def copy(src, dst, device):
        sem = used[0]
        used[0] += 1
        return pltpu.make_async_remote_copy(
            src_ref=src,
            dst_ref=dst,
            send_sem=n.send_sem.at[sem],
            recv_sem=n.recv_sem.at[sem],
            device_id=device,
            device_id_type=MESH,
        )

    barrier = pltpu.get_barrier_semaphore()
    friends = [partner]
    if inside:
        friends.append(sibling)
        for offset in range(1, 8):
            place = 2 * ((me // 2 + offset) % 8) + core
            friends += [(me_pair, place), (other, place)]
    loads = [
        pltpu.make_async_copy(src, dst, n.load_sem.at[i])
        for i, (src, dst) in enumerate(
            (
                (n.hbm_qkv, n.w_qkv),
                (n.hbm_out, n.w_out),
                (n.hbm_up, n.w_up),
                (n.hbm_down, n.w_down),
                (n.hbm_head, n.w_head),
            )
        )
    ]
    for load in loads:
        load.start()
    for friend in friends:
        pl.semaphore_signal(barrier, inc=1, device_id=friend, device_id_type=MESH)

    weights = {QKV: n.w_qkv, OUT: n.w_out, UP: n.w_up, DOWN: n.w_down, HEAD: n.w_head}

    def piece_of(ref, half):
        height = ref.shape[0] // data_count
        width = ref.shape[1] // 2
        return (
            pl.ds(pl.multiple_of(me * height, height), height),
            pl.ds(pl.multiple_of(half * width, width), width),
        )

    weight_copies = {}
    if inside:
        for name, ref in weights.items():
            weight_copies[name] = copy(
                ref.at[piece_of(ref, other)], getattr(n, "their_" + name), partner
            )
        weight_copies[GAINS] = copy(n.gains, n.their_gains, partner)

    count_copies = []
    if inside:
        count_copies.append(copy(n.count_out.at[0], n.count_in.at[0], sibling))
        for offset in range(1, 8):
            place = (me // 2 + offset) % 8
            count_copies.append(
                copy(n.count_out.at[1], n.count_in.at[offset], (me_pair, 2 * place + core))
            )

    n.gain_sums[...] = jnp.zeros_like(n.gain_sums)
    lay_out_inputs(n, seq_count)
    loads[0].wait()

    @pl.loop(0, seq_count // 2)
    def _(t):
        forward_sequences(n, 2 * t, online, loads[1:])

        @pl.when(t == 0)
        def _():
            pl.semaphore_wait(barrier, len(friends))
            if not inside:
                return
            n.count_out[0] = jnp.broadcast_to(
                jnp.sum(n.table[...], axis=0, keepdims=True), (8, 128)
            )
            count_copies[0].start()
            for each in weight_copies.values():
                each.start()

        @pl.when(t == 1)
        def _():
            if not inside:
                return
            count_copies[0].wait()
            n.count_out[1] = n.count_out[0] + n.count_in[0]
            for each in count_copies[1:]:
                each.start()

    lane = lax.broadcasted_iota(jnp.int32, (8, LP), 1)
    seq = lax.broadcasted_iota(jnp.int32, (8, LP), 0)
    real = jnp.logical_and(lane < L, seq < seq_count)
    tops = n.tops[...]
    aims_copy = copy(n.aims_out, n.aims_in, partner)
    q_copy = copy(n.q_rows.at[:, :, pl.ds(128, 128)], n.q_half, partner)
    state_sem = used[0]
    used[0] += seq_count

    def state_copy(s):
        return pltpu.make_async_remote_copy(
            src_ref=n.grad_states.at[s, :, pl.ds(d // 2, d // 2)],
            dst_ref=n.state_half.at[s],
            send_sem=n.send_sem.at[state_sem + s],
            recv_sem=n.recv_sem.at[state_sem + s],
            device_id=partner,
            device_id_type=MESH,
        )

    @pl.when(jnp.logical_not(online))
    def _():
        reward = jnp.concatenate([n.aux[s, 1:2, :] for s in range(seq_count)] * 2, axis=0)
        finished = jnp.concatenate([n.aux[s, 2:3, :] for s in range(seq_count)] * 2, axis=0)
        n.aims_out[...] = reward + DISCOUNT * (1.0 - finished) * tops
        aims_copy.start()

    @pl.when(online)
    def _():
        q_copy.start()

    if inside:
        for name, each in weight_copies.items():
            each.wait()
            if name == GAINS:
                mine, received = n.gains[...], n.their_gains[...]
            else:
                mine = weights[name][piece_of(weights[name], me_pair)].astype(F32)
                received = getattr(n, "their_" + name)[...].astype(F32)
            first = jnp.where(online, mine, received)
            second = jnp.where(online, received, mine)
            getattr(n, "new_" + name)[...] = second + SOFT_RATE * (first - second)
        counts = n.count_out[1]
        for i in range(1, 8):
            count_copies[i].wait()
            counts += n.count_in[i]
    else:
        counts = n.counts[...]
    seq_weight = (seq_count * data_count) / (
        TASKS * jnp.sum(n.table[...] * counts, axis=1, keepdims=True)
    )

    stat_row_id = lax.broadcasted_iota(jnp.int32, (8, 128), 0)
    stat_lane = lax.broadcasted_iota(jnp.int32, (8, 128), 1)
    stat_axes = ("core", ROW, LOW, HIGH, PAIR)
    stat_copies = [] if not inside else [
        copy(n.stat_out.at[i], n.stat_in.at[i], across[axis]) for i, axis in enumerate(stat_axes)
    ]

    def stat_first(loss):
        total = jnp.sum(jnp.where(real, tops, 0.0))
        best = jnp.max(jnp.where(real, tops, LOWEST))
        sums = jnp.where(stat_lane == 0, loss, jnp.where(stat_lane == 1 + me_pair, total, 0.0))
        bests = jnp.where(stat_lane == me_pair, best, LOWEST)
        n.stat_out[0] = jnp.where(stat_row_id == 0, sums, jnp.where(stat_row_id == 1, bests, 0.0))
        if inside:
            stat_copies[0].start()

    def stat_next(i):
        if not inside:
            return
        stat_copies[i].wait()
        mine, received = n.stat_out[i], n.stat_in[i]
        joined = jnp.where(stat_row_id == 1, jnp.maximum(mine, received), mine + received)
        n.stat_out[i + 1] = joined
        if i + 1 < len(stat_copies):
            stat_copies[i + 1].start()

    def half_of(name, half):
        if name in CHUNKS:
            first, second = (128 * len(at) for at in CHUNKS[name])
            return (slice(None), pl.ds(first * half, second if half else first))
        ref = getattr(n, "r1_" + name)
        height, width = (size // 2 for size in ref.shape[-2:])
        if name == DOWN:
            return (pl.ds(half * height, height), slice(None))
        return (slice(None), pl.ds(half * width, width))

    def put(name, total, pair=0):
        if name in CHUNKS:
            for i, at in enumerate(CHUNKS[name][pair]):
                n.grad_qkv[:, at : at + 128] = total[:, 128 * i : 128 * i + 128]
        elif name in (UP_A, UP_B):
            width = total.shape[1]
            n.grad_up[:, pl.ds(width * (name == UP_B), width)] = total
        else:
            getattr(n, "grad_" + name)[...] = total

    def places(count):
        if count == 0:
            return [()]
        return [(i,) + rest for i in range(2) for rest in places(count - 1)]

    def index_at(left, axis, value, place=None):
        place = iter(place or (slice(None),) * 2)
        return tuple(value if each == axis else next(place) for each in left)

    def left_after(name, count):
        return tuple(each for each in AXES if each not in ROUTES[name][:count])

    def n_far(name):
        return getattr(n, "far_" + name)

    core_copies, axis_copies, far_copies, pair_copies = {}, {}, {}, {}
    for name in ROUTES if inside else ():
        r1 = getattr(n, "r1_" + name)
        core_copies[name] = copy(getattr(n, "g_" + name).at[:, :, :, 1 - core], r1, sibling)
        if name == DOWN:
            whole = (slice(None),) * 3
            pair_copies[name] = copy(r1.at[whole + half_of(name, 1)], n.half_down, partner)
            r1 = n.half_down
        axis_copies[name] = []
        for i, axis in enumerate(ROUTES[name]):
            src = r1 if i == 0 else getattr(n, f"r{i + 1}_{name}")
            view = src.at[index_at(left_after(name, i), axis, 1 - bits[axis])]
            axis_copies[name].append(copy(view, getattr(n, f"r{i + 2}_{name}"), across[axis]))
        if len(ROUTES[name]) == 1:
            rest = left_after(name, 1)
            mine = 2 * bits[rest[0]] + bits[rest[1]]
            far_copies[name] = []
            for k in range(7 if name in CHUNKS else 3):
                offset, pair = (k + 1) % 4, 0 if k < 3 else 1
                place = (mine + offset) % 4
                target = me
                for each, bit in zip(rest, (place // 2, place % 2)):
                    target = target + STRIDES[each] * (bit - bits[each])
                view, landing = (place // 2, place % 2), (offset,)
                if name in CHUNKS:
                    view += half_of(name, pair)
                    landing += (slice(None), pl.ds(0, 128 * len(CHUNKS[name][pair])))
                else:
                    pair = me_pair
                far_copies[name].append(
                    copy(getattr(n, "r2_" + name).at[view], n_far(name).at[landing], (pair, target))
                )
        if name != DOWN and name not in CHUNKS:
            pair_copies[name] = copy(getattr(n, "to_" + name), getattr(n, "from_" + name), partner)

    def core_start(name):
        if inside:
            core_copies[name].start()

    def core_done(name):
        if not inside:
            return
        core_copies[name].wait()
        g, r1 = getattr(n, "g_" + name), getattr(n, "r1_" + name)
        for place in places(3):
            total = (g[place + (core,)].astype(F32) + r1[place].astype(F32)).astype(BF16)
            if name == DOWN:
                height = total.shape[0] // 2
                n.half_down[place] = total[:height]
                r1[place + half_of(name, 1)] = total[height:]
            else:
                r1[place] = total
        if name == DOWN:
            pair_copies[name].start()
        axis_copies[name][0].start()

    def axis_done(name, i=0):
        if not inside:
            return
        axis = ROUTES[name][i]
        left = left_after(name, i)
        axis_copies[name][i].wait()
        src = n.half_down if name == DOWN else getattr(n, f"r{i + 1}_{name}")
        dst = getattr(n, f"r{i + 2}_{name}")
        for place in places(len(left) - 1):
            mine = src[index_at(left, axis, bits[axis], place)].astype(F32)
            at = place or (slice(None),) * 2
            total = mine + dst[at].astype(F32)
            if place:
                dst[at] = total.astype(BF16)
        if i + 1 < len(ROUTES[name]):
            axis_copies[name][i + 1].start()
        elif len(left) == 1:
            to_pair(name, total)
        else:
            for each in far_copies[name]:
                each.start()

    def to_pair(name, total):
        width = total.shape[1] // 2
        getattr(n, "to_" + name)[...] = total[:, width:].astype(BF16)
        pair_copies[name].start()
        put(name, total[:, :width])

    def far_total(name, pair):
        r2, far = getattr(n, "r2_" + name), n_far(name)
        total = None
        if pair == 0 or name == DOWN:
            first, second = left_after(name, 1)
            view = (bits[first], bits[second])
            total = r2[view + half_of(name, 0) if name in CHUNKS else view].astype(F32)
        for k in range(3) if pair == 0 or name == DOWN else range(3, 7):
            far_copies[name][k].wait_recv()
            part = far[(k + 1) % 4]
            if name in CHUNKS:
                part = part[:, : 128 * len(CHUNKS[name][pair])]
            part = part.astype(F32)
            total = part if total is None else total + part
        return total

    def far_done(name):
        if not inside:
            return
        total = far_total(name, 0)
        if name in pair_copies and name != DOWN:
            to_pair(name, total)
        else:
            put(name, total)

    def far_done_target(name):
        if not inside:
            return
        if name in CHUNKS:
            total = far_total(name, 1)
        elif name == DOWN:
            pair_copies[name].wait_recv()
            axis_copies[name][0].start()
            axis_done(name)
            total = far_total(name, 1)
        else:
            pair_copies[name].wait_recv()
            total = getattr(n, "from_" + name)[...].astype(F32)
        put(name, total, 1)

    gain_copies = []
    if inside:
        gain_copies = [
            copy(n.gain_out.at[0], n.gain_in.at[0], sibling),
            copy(n.gain_out.at[1], n.gain_in.at[1], across[ROW]),
        ]
        for k in range(7):
            offset, pair = (k + 1) % 4, 0 if k < 3 else 1
            gain_copies.append(
                copy(
                    n.gain_out.at[2],
                    n.gain_in.at[2 + offset],
                    at_quarter((quarter + offset) % 4, pair),
                )
            )

    def gain_step(i):
        if not inside:
            return
        gain_copies[i].wait()
        n.gain_out[i + 1] = n.gain_out[i] + n.gain_in[i]
        for each in gain_copies[1:2] if i == 0 else gain_copies[2:]:
            each.start()

    def gain_owner(pair):
        if not inside:
            n.grad_gains[...] = n.gain_out[0]
            return
        total = n.gain_out[2] if pair == 0 else None
        for k in range(3) if pair == 0 else range(3, 7):
            gain_copies[2 + k].wait_recv()
            part = n.gain_in[2 + (k + 1) % 4]
            total = part if total is None else total + part
        n.grad_gains[...] = total

    def turned(ref):
        return jnp.transpose(rows_of(ref, 0, d))

    def product(left, right):
        return dot_nn(left[...], right.reshape(seq_count * LP, right.shape[2]))

    def blocks(value):
        return value.astype(BF16).reshape(2, 2, 2, 2, d // 16, value.shape[1])

    @pl.when(online)
    def _():
        n.turned_one[...] = turned(n.normed_one)
        n.turned_two[...] = turned(n.normed_two)
        n.turned_mixed[...] = turned(n.attended)
        aims_copy.wait_recv()
        differ = n.picked[...] - n.aims_in[...]
        weighted = jnp.where(real, seq_weight * differ, 0.0)
        n.coef[...] = weighted
        stat_first(jnp.sum(0.5 * weighted * jnp.where(real, differ, 0.0)))

        @pl.loop(0, seq_count)
        def _(s):
            backward_head(n, s)

        n.turned_ffn[...] = turned(n.grad_ffn)

        @pl.loop(0, ff // 512)
        def _(j):
            columns = pl.ds(pl.multiple_of(j * 512, 512), 512)
            value = product(n.turned_ffn, n.active[:, :, columns]).astype(BF16)
            for c in range(4):
                n.g_down[j // 2, j % 2, c // 2, c % 2] = value[:, 128 * c : 128 * c + 128]

        core_start(DOWN)
        value = None
        for s in range(seq_count):
            part = dot_nn(n.grad_q[s], n.final_low[s])
            value = part if value is None else value + part
        n.g_head[...] = blocks(jnp.transpose(value))
        core_start(HEAD)
        stat_next(0)

        @pl.loop(0, seq_count // 2)
        def _(t):
            backward_upper(n, 2 * t)

        core_done(DOWN)
        core_done(HEAD)

        def up_product(ref, tiles, first):
            @pl.loop(0, 2 * tiles)
            def _(j):
                columns = pl.ds(
                    pl.multiple_of((j // tiles) * (ff // 2) + first + (j % tiles) * 512, 512), 512
                )
                here = pl.ds(pl.multiple_of(j * 512, 512), 512)
                ref[:, :, :, :, :, here] = blocks(product(n.turned_two, n.slope[:, :, columns]))

        if inside:
            up_product(n.g_up_a, ff // 4 // 512, 0)
            core_start(UP_A)
            up_product(n.g_up_b, ff // 4 // 512, ff // 4)
            core_start(UP_B)
        else:
            up_product(n.g_up, ff // 2 // 512, 0)
        stat_next(1)

        @pl.loop(0, seq_count // 2)
        def _(t):
            backward_middle(n, 2 * t)

            @pl.when(t == 0)
            def _():
                core_done(UP_A)

            @pl.when(t == 1)
            def _():
                core_done(UP_B)

        n.g_out[...] = blocks(product(n.turned_mixed, n.grad_branch[...]))
        core_start(OUT)
        stat_next(2)

        @pl.loop(0, seq_count)
        def _(s):
            attend_back(n, [(s, pair) for pair in range(d // 128)], d)
            backward_states(n, s)
            state_copy(s).start()

            @pl.when(s == 0)
            def _():
                axis_done(DOWN)
                axis_done(HEAD)
                core_done(OUT)

            @pl.when(s == 1)
            def _():
                stat_next(3)
                axis_done(UP_A)

            @pl.when(s == 2)
            def _():
                axis_done(UP_B)

            @pl.when(s == 3)
            def _():
                axis_done(OUT)
                far_done(HEAD)
                axis_done(UP_A, 1)

        n.gain_out[0, 0:1, :] = jnp.sum(n.gain_sums[0], axis=0, keepdims=True)
        n.gain_out[0, 1:2, :] = jnp.sum(n.gain_sums[1], axis=0, keepdims=True)
        n.gain_out[0, 2:8, :] = jnp.zeros((6, d), F32)

        def qkv_product(first, *names):
            width = 256 // len(names)
            for half in range(2):
                at = half * (3 * d // 2) + first
                value = blocks(product(n.turned_one, n.qkv[:, :, at : at + 256]))
                for i, name in enumerate(names):
                    getattr(n, "g_" + name)[..., half * width : (half + 1) * width] = value[
                        ..., i * width : (i + 1) * width
                    ]
            for name in names:
                core_start(name)

        if inside:
            gain_copies[0].start()
            qkv_product(0, QKV_0)
            axis_done(UP_B, 1)
            qkv_product(256, QKV_1)
            core_done(QKV_0)
            qkv_product(512, QKV_2, QKV_3)
            core_done(QKV_1)
            core_done(QKV_2)
            core_done(QKV_3)
            gain_step(0)
            far_done(DOWN)
            axis_done(UP_A, 2)
        else:
            for first in range(0, 3 * d, 256):
                n.g_qkv[..., first : first + 256] = blocks(
                    product(n.turned_one, n.qkv[:, :, first : first + 256])
                )
        for s in range(0, seq_count, 2):
            n.state_out[s * L : (s + 2) * L] = without_pad(n.grad_states, s, d // 2)
            n.q_out[s * L : (s + 2) * L] = without_pad(n.q_rows, s, 128)
        axis_done(QKV_0)
        if inside:
            gain_step(1)
        axis_done(QKV_1)
        axis_done(QKV_2)
        axis_done(QKV_3)
        far_done(OUT)
        axis_done(UP_B, 2)
        gain_owner(0)
        for name in CHUNKS:
            far_done(name)
        q_copy.wait_send()
        for s in range(seq_count):
            state_copy(s).wait_send()
        for each in pair_copies.values():
            each.wait_send()
        for each in gain_copies[2:] + [each for sent in far_copies.values() for each in sent]:
            each.wait_send()

    @pl.when(jnp.logical_not(online))
    def _():
        stat_first(0.0)
        for i in range(4):
            stat_next(i)
        far_done_target(DOWN)
        q_copy.wait_recv()
        for s in range(0, seq_count, 2):
            n.q_out[s * L : (s + 2) * L] = without_pad(n.q_half, s, 128)
        for s in range(seq_count):
            state_copy(s).wait_recv()
            if s % 2:
                n.state_out[(s - 1) * L : (s + 1) * L] = without_pad(n.state_half, s - 1, d // 2)
        for name in (HEAD, UP_A, UP_B, OUT):
            far_done_target(name)
        if inside:
            gain_owner(1)
        for name in CHUNKS:
            far_done_target(name)
        aims_copy.wait_send()
        if inside:
            for each in far_copies[DOWN]:
                each.wait_send()

    if inside:
        stat_next(4)
        n.stats[...] = n.stat_out[5]
    else:
        n.stats[...] = n.stat_out[0]
    assert used[0] <= SEMAPHORES


OUTPUTS = (
    "q_out",
    "state_out",
    GRAD_GAINS,
    "grad_qkv",
    "grad_out",
    "grad_up",
    GRAD_DOWN,
    "grad_head",
    NEW_GAINS,
    "new_qkv",
    "new_out",
    "new_up",
    "new_down",
    "new_head",
    STATS,
)


def finish_kernel(moved, worked, token_total, data_count, *refs):
    source = dict(zip(moved + worked, refs))
    result = dict(zip(OUTPUTS, refs[len(source) :]))
    sems = refs[-1]
    copies = [
        pltpu.make_async_copy(source[name], result[name], sems.at[i])
        for i, name in enumerate(moved)
    ]
    for copy in copies:
        copy.start()
    me_pair = lax.axis_index(PAIR)
    me = lax.axis_index(DP)
    for name in (GRAD_GAINS, NEW_GAINS):
        height = source[name].shape[1] // data_count
        here = source[name][:, pl.ds(pl.multiple_of(me * height // 128 * 128, 128), 128)]
        value = here[:, :height]
        for at in range(height, 128, height):
            value = jnp.where(me * height % 128 == at, here[:, at : at + height], value)
        result[name][...] = jnp.where(me_pair == 0, value[0:1], value[1:2])
    if GRAD_DOWN in worked:
        result[GRAD_DOWN][...] = jnp.transpose(source[GRAD_DOWN][...])
    stats = source[STATS]
    result[STATS][0] = stats[0, 0] / token_total
    result[STATS][1] = stats[0, 1] / token_total
    result[STATS][2] = stats[1, 0]
    result[STATS][3] = stats[0, 2] / token_total
    result[STATS][4] = stats[1, 1]
    for copy in copies:
        copy.wait()


def add_outside(out, params, pair_index, data_index, data_count):
    online = pair_index == 0
    other = 1 - pair_index

    def half(matrix, which):
        width = matrix.shape[1] // 2
        return lax.dynamic_slice_in_dim(matrix, which * width, width, 1)

    def piece(matrix, which):
        height = matrix.shape[0] // data_count
        return half(lax.dynamic_slice_in_dim(matrix, data_index * height, height, 0), which)

    def swapped(value):
        return lax.ppermute(value, PAIR, [(0, 1), (1, 0)])

    for name in TENSORS:
        grad = out["g_" + name].astype(F32)
        grad = grad.reshape((16,) + grad.shape[4:])
        if name == DOWN:
            grad = jnp.swapaxes(grad, 1, 2)
        grad = lax.psum_scatter(
            grad.reshape(-1, grad.shape[2]), DP, scatter_dimension=0, tiled=True
        )
        received = swapped(half(grad, other))
        out["grad_" + name] = jnp.where(online, half(grad, pair_index), received)
    gains = lax.psum(out[GRAD_GAINS], DP)
    out[GRAD_GAINS] = jnp.where(online, gains, swapped(gains))
    for name, weight in zip((GAINS, QKV, OUT, UP, DOWN, HEAD), params):
        if name == GAINS:
            weight = jnp.pad(weight.T, ((0, 6), (0, 0)))
            mine, received = weight.astype(F32), swapped(weight).astype(F32)
        else:
            mine = piece(weight, pair_index).astype(F32)
            received = swapped(piece(weight, other)).astype(F32)
        first, second = jnp.where(online, mine, received), jnp.where(online, received, mine)
        out["new_" + name] = second + SOFT_RATE * (first - second)
    sums = lax.psum(out[STATS][0:1], (PAIR, DP))
    bests = lax.pmax(out[STATS][1:2], (PAIR, DP))
    out[STATS] = jnp.concatenate([sums, bests])


def local(
    states, norm_gains, w_qkv, w_out, w_up, w_down, w_head, task_ids, chosen, reward, finished
):
    pair_index = lax.axis_index(PAIR)
    data_index = lax.axis_index(DP)
    data_count = lax.axis_size(DP)
    row_count, d = states.shape[1:]
    ff = w_up.shape[2]
    bin_count = w_head.shape[2]
    seq_count = row_count // L

    inside = data_count == 16
    rows = (seq_count, LP, d)
    inputs = dict(
        states=states[0],
        norm_gains=norm_gains[0].T,
        hbm_qkv=w_qkv[0],
        hbm_out=w_out[0],
        hbm_up=w_up[0],
        hbm_down=w_down[0],
        hbm_head=w_head[0],
        task_ids=task_ids,
        chosen=chosen,
        reward=reward,
        finished=finished,
    )
    if not inside:
        table = (task_ids[:, None] == jnp.arange(128, dtype=jnp.int32)[None, :]).astype(F32)
        inputs["counts"] = jnp.broadcast_to(
            lax.psum(jnp.sum(table, axis=0, keepdims=True), DP), (8, 128)
        )
    piece = {
        QKV: (d // 16, 3 * d),
        OUT: (d // 16, d),
        UP: (d // 16, ff),
        HEAD: (d // 16, bin_count),
        DOWN: (d, ff // 16),
    }
    halves = {
        name: (shape[0] // 2, shape[1]) if name == DOWN else (shape[0], shape[1] // 2)
        for name, shape in piece.items()
    }
    new_shapes = dict(halves, down=(ff // 16, d // 2))
    outputs = dict(
        q_out=((row_count, bin_count // 2), BF16),
        state_out=((row_count, d // 2), BF16),
        grad_gains=((8, d), F32),
        new_gains=((8, d), F32),
        stats=((8, 128), F32),
    )
    for name in TENSORS:
        if inside:
            outputs["grad_" + name] = (halves[name], F32)
            outputs["new_" + name] = (new_shapes[name], F32)
        else:
            outputs["g_" + name] = ((2, 2, 2, 2) + piece[name], BF16)
    scratch = dict(
        w_qkv=((d, 3 * d), BF16),
        w_out=((d, d), BF16),
        w_up=((d, ff), BF16),
        w_down=((ff, d), BF16),
        w_head=((d, bin_count), BF16),
        x=(rows, BF16),
        gains=((8, d), F32),
        flat=((8, -(-(row_count + LP - L) // 128) * 128), F32),
        aux=((seq_count, 8, LP), F32),
        table=((8, 128), F32),
        normed_one=(rows, BF16),
        qkv=((seq_count, LP, 3 * d), BF16),
        powers_0=((seq_count, d // 128) + (2 * BLOCKS[0][1], BLOCKS[0][2]), BF16),
        powers_1=((seq_count, d // 128) + (2 * BLOCKS[1][1], BLOCKS[1][2]), BF16),
        powers_2=((seq_count, d // 128) + (2 * BLOCKS[2][1], BLOCKS[2][2]), BF16),
        inverse_totals=(rows, F32),
        attended=(rows, BF16),
        middle=(rows, F32),
        normed_two=(rows, BF16),
        active=((seq_count, LP, ff), BF16),
        slope=((seq_count, LP, ff), BF16),
        final_low=(rows, BF16),
        q_rows=((seq_count, LP, bin_count), BF16),
        q_half=((seq_count, LP, bin_count // 2), BF16),
        picked=((8, LP), F32),
        tops=((8, LP), F32),
        coef=((8, LP), F32),
        aims_out=((8, LP), F32),
        aims_in=((8, LP), F32),
        grad_q=((seq_count, bin_count, LP), BF16),
        grad_ffn=(rows, BF16),
        turned_one=((d, seq_count * LP), BF16),
        turned_two=((d, seq_count * LP), BF16),
        turned_mixed=((d, seq_count * LP), BF16),
        turned_ffn=((d, seq_count * LP), BF16),
        state_half=((seq_count, LP, d // 2), BF16),
        gain_sums=((2, 8, d), F32),
        gain_out=((3, 8, d), F32),
        gain_in=((6, 8, d), F32),
        count_out=((2, 8, 128), F32),
        count_in=((8, 8, 128), F32),
        stat_out=((6, 8, 128), F32),
        stat_in=((5, 8, 128), F32),
        their_gains=((8, d), F32),
    )
    if inside:
        for name in TENSORS:
            scratch["their_" + name] = (new_shapes[name], BF16)
        scratch["half_down"] = ((2, 2, 2) + halves[DOWN], BF16)
        for name, route in ROUTES.items():
            if name in CHUNKS:
                far = (d // 16, 128 * len(CHUNKS[name][0]))
                shape = (far[0], 2 * far[1])
            elif name == DOWN:
                shape, far = piece[DOWN], halves[DOWN]
            else:
                shape = far = (d // 16, ff // 2) if name in (UP_A, UP_B) else piece[name]
                scratch["to_" + name] = (shape[0], shape[1] // 2), BF16
                scratch["from_" + name] = (shape[0], shape[1] // 2), BF16
            scratch["g_" + name] = ((2, 2, 2, 2) + shape, BF16)
            scratch["r1_" + name] = ((2, 2, 2) + shape, BF16)
            for i in range(len(route)):
                scratch[f"r{i + 2}_{name}"] = ((2,) * (2 - i) + (far if name == DOWN else shape), BF16)
            if len(route) == 1:
                scratch["far_" + name] = ((4,) + far, BF16)
    names = list(inputs) + list(outputs) + list(scratch) + ["send_sem", "recv_sem", "load_sem"]
    in_vmem = pl.BlockSpec(memory_space=pltpu.VMEM)
    in_smem = pl.BlockSpec(memory_space=pltpu.SMEM)
    anywhere = pl.BlockSpec(memory_space=pl.ANY)
    raw = pl.pallas_call(
        functools.partial(layer_kernel, names, data_count, inside),
        out_shape=[jax.ShapeDtypeStruct(shape, dtype) for shape, dtype in outputs.values()],
        in_specs=[
            in_smem if name == "task_ids" else anywhere if name[:3] == "hbm" else in_vmem
            for name in inputs
        ],
        out_specs=[in_vmem] * len(outputs),
        scratch_shapes=[pltpu.VMEM(shape, dtype) for shape, dtype in scratch.values()]
        + [pltpu.SemaphoreType.DMA((SEMAPHORES,)), pltpu.SemaphoreType.DMA((SEMAPHORES,))]
        + [pltpu.SemaphoreType.DMA((5,))],
        compiler_params=pltpu.CompilerParams(
            collective_id=0, has_side_effects=True, vmem_limit_bytes=64 * 1024 * 1024 - 65536
        ),
        name="layer",
    )(*inputs.values())
    out = dict(zip(outputs, raw))
    if not inside:
        params = (norm_gains[0], w_qkv[0], w_out[0], w_up[0], w_down[0], w_head[0])
        add_outside(out, params, pair_index, data_index, data_count)
    moved = {name: out[name] for name in OUTPUTS if name not in (GRAD_GAINS, NEW_GAINS, STATS)}
    worked = {name: out[name] for name in (GRAD_GAINS, NEW_GAINS, STATS)}
    results = {name: jax.ShapeDtypeStruct(value.shape, value.dtype) for name, value in moved.items()}
    if inside:
        worked[GRAD_DOWN] = moved.pop(GRAD_DOWN)
        results[GRAD_DOWN] = jax.ShapeDtypeStruct((ff // data_count, d // 2), F32)
    results[GRAD_GAINS] = results[NEW_GAINS] = jax.ShapeDtypeStruct((1, d // data_count), F32)
    results[STATS] = jax.ShapeDtypeStruct((5,), F32)
    spec_of = {name: anywhere if name in moved else in_vmem for name in OUTPUTS}
    spec_of[STATS] = in_smem
    final = pl.pallas_call(
        functools.partial(
            finish_kernel, list(moved), list(worked), row_count * data_count, data_count
        ),
        out_shape=[results[name] for name in OUTPUTS],
        in_specs=[in_vmem] * (len(moved) + len(worked)),
        out_specs=[spec_of[name] for name in OUTPUTS],
        scratch_shapes=[
            pltpu.SemaphoreType.DMA((len(moved),)),
        ],
        name="finish",
    )(*moved.values(), *worked.values())
    final = dict(zip(OUTPUTS, final))
    for name in (GRAD_GAINS, NEW_GAINS):
        final[name] = final[name].T
    return tuple(final.values())


def solution(mesh):
    placed = (
        P(PAIR, DP, None),
        P(PAIR, None, None),
        P(PAIR, None, None),
        P(PAIR, None, None),
        P(PAIR, None, None),
        P(PAIR, None, None),
        P(PAIR, None, None),
        P(DP),
        P(DP),
        P(DP),
        P(DP),
    )
    return jax.shard_map(
        local,
        mesh=mesh,
        in_specs=placed,
        out_specs=(P(DP, PAIR),) * 14 + (P(),),
        check_vma=False,
    )
```

time: 104 us -> 91.5 us (0.88)
  Pallas kernels: 103 us -> 90.5 us
    pallas_call x1, Pallas kernels: 99.7 us -> 87.1 us  [local(): pl.pallas_call(functools.partial(layer_kernel, names, data_count, inside)...]
where the time goes in v3:
time: 91.5 us; the launch traced here: 91.3 us
  Pallas kernels  90.5 us (99%)
    pallas_call x1, Pallas kernels, local(): pl.pallas_call(functools.partial(layer_kernel, names, data_count, inside)...  87.1 us
    pallas_call x1, Pallas kernels, local(): pl.pallas_call(functools.partial(finish_kernel, list(moved), list(worked)...  3.38 us

profile of v3, /device:TPU:0, one launch (start us, length us, event | category | flops | bytes accessed | tf_op | source)
XLA Modules:
  0.0 91.3 jit_solution(16679651866392172238)
XLA Ops:
  0.6 87.1 %layer.1 = (bf16[1184,128]{1,0:T(8,128)(2,1)}, bf16[1184,256]{1,0:T(8,128)(2,1)}, f32[8,512]{1,0:T(8,128)}, f32[8,512]{1,0:T(8,128)}, f32[8,128]{1,0:T(8,128)}, ...) custom-call(bf16[1184,512]{1,0:T(8,128)(2,1)} %bitcast.14, ...), custom_call_target="tpu_custom_call" | custom-call | tf_op jit(solution)/shard_map/layer/pallas_call | solution.py:1208
  87.8 3.4 %finish.1 = (bf16[1184,128]{1,0:T(8,128)(2,1)}, bf16[1184,256]{1,0:T(8,128)(2,1)}, f32[1,32]{1,0:T(1,128)}, f32[32,768]{1,0:T(8,128)}, f32[32,256]{1,0:T(8,128)}...) custom-call(bf16[1184,128]{1,0:T(8,128)(2,1)} %get-tuple-element.45., ...), custom_call_target="tpu_custom_call" | custom-call | tf_op jit(solution)/shard_map/finish/pallas_call | solution.py:1238

commit v4 on v3

--- a/solution.py
+++ b/solution.py
@@ -370,26 +370,21 @@
 
 
 ROUTES = {
-    DOWN: (ROW,),
-    HEAD: (ROW,),
-    UP_A: (ROW, LOW, HIGH),
-    UP_B: (LOW, ROW, HIGH),
-    OUT: (ROW,),
-    QKV_0: (ROW,),
-    QKV_1: (LOW,),
-    QKV_2: (ROW,),
-    QKV_3: (LOW,),
+    DOWN: ((), (ROW,)),
+    HEAD: ((ROW,), ()),
+    UP_A: ((ROW, LOW), (HIGH,)),
+    UP_B: ((LOW, ROW), (HIGH,)),
+    OUT: ((ROW,), ()),
+    QKV_0: ((ROW,), ()),
+    QKV_1: ((LOW,), ()),
+    QKV_2: ((ROW,), ()),
+    QKV_3: ((LOW,), ()),
 }
-CHUNKS = {
-    QKV_0: ((0, 128), (0, 128)),
-    QKV_1: ((256, 384), (256, 384)),
-    QKV_2: ((512,), (512,)),
-    QKV_3: ((640,), (640,)),
-}
+CHUNKS = {QKV_0: (0, 256), QKV_1: (256, 512), QKV_2: (512, 640), QKV_3: (640, 768)}
 STRIDES = {HIGH: 8, LOW: 4, ROW: 2}
 TENSORS = (DOWN, HEAD, UP, OUT, QKV)
 AXES = (HIGH, LOW, ROW)
-SEMAPHORES = 128
+SEMAPHORES = 160
 
 
 def layer_kernel(names, data_count, inside, *refs):
@@ -597,19 +592,15 @@
             stat_copies[i + 1].start()
 
     def half_of(name, half):
-        if name in CHUNKS:
-            first, second = (128 * len(at) for at in CHUNKS[name])
-            return (slice(None), pl.ds(first * half, second if half else first))
-        ref = getattr(n, "r1_" + name)
-        height, width = (size // 2 for size in ref.shape[-2:])
+        height, width = (size // 2 for size in getattr(n, "r1_" + name).shape[-2:])
         if name == DOWN:
             return (pl.ds(half * height, height), slice(None))
         return (slice(None), pl.ds(half * width, width))
 
-    def put(name, total, pair=0):
+    def put(name, total):
         if name in CHUNKS:
-            for i, at in enumerate(CHUNKS[name][pair]):
-                n.grad_qkv[:, at : at + 128] = total[:, 128 * i : 128 * i + 128]
+            first, last = CHUNKS[name]
+            n.grad_qkv[:, first:last] = total
         elif name in (UP_A, UP_B):
             width = total.shape[1]
             n.grad_up[:, pl.ds(width * (name == UP_B), width)] = total
@@ -625,168 +616,164 @@
         place = iter(place or (slice(None),) * 2)
         return tuple(value if each == axis else next(place) for each in left)
 
-    def left_after(name, count):
-        return tuple(each for each in AXES if each not in ROUTES[name][:count])
-
-    def n_far(name):
-        return getattr(n, "far_" + name)
-
-    core_copies, axis_copies, far_copies, pair_copies = {}, {}, {}, {}
-    for name in ROUTES if inside else ():
-        r1 = getattr(n, "r1_" + name)
-        core_copies[name] = copy(getattr(n, "g_" + name).at[:, :, :, 1 - core], r1, sibling)
-        if name == DOWN:
-            whole = (slice(None),) * 3
-            pair_copies[name] = copy(r1.at[whole + half_of(name, 1)], n.half_down, partner)
-            r1 = n.half_down
-        axis_copies[name] = []
-        for i, axis in enumerate(ROUTES[name]):
-            src = r1 if i == 0 else getattr(n, f"r{i + 1}_{name}")
-            view = src.at[index_at(left_after(name, i), axis, 1 - bits[axis])]
-            axis_copies[name].append(copy(view, getattr(n, f"r{i + 2}_{name}"), across[axis]))
-        if len(ROUTES[name]) == 1:
-            rest = left_after(name, 1)
-            mine = 2 * bits[rest[0]] + bits[rest[1]]
-            far_copies[name] = []
-            for k in range(7 if name in CHUNKS else 3):
-                offset, pair = (k + 1) % 4, 0 if k < 3 else 1
+    def left_after(done):
+        return tuple(each for each in AXES if each not in done)
+
+    def exchange(src, dst, left, axis):
+        view = src.at[index_at(left, axis, 1 - bits[axis])]
+        return copy(view, dst, across[axis])
+
+    core_copies, before, pair_copies, after, straight = {}, {}, {}, {}, {}
+    for name, (first_axes, then_axes) in ROUTES.items() if inside else ():
+        ref = getattr(n, "r1_" + name)
+        core_copies[name] = copy(getattr(n, "g_" + name).at[:, :, :, 1 - core], ref, sibling)
+        left = AXES
+        before[name] = []
+        for i, axis in enumerate(first_axes):
+            dst = getattr(n, f"r{i + 2}_{name}")
+            before[name].append((ref, dst, left, axis, exchange(ref, dst, left, axis)))
+            ref, left = dst, left_after(first_axes[: i + 1])
+        whole = (slice(None),) * len(left)
+        half = getattr(n, "half_" + name)
+        pair_copies[name] = copy(ref.at[whole + half_of(name, 1)], half, partner)
+        after[name] = []
+        ref = half
+        for i, axis in enumerate(then_axes):
+            dst = getattr(n, "then_" + name)
+            after[name].append((ref, dst, left, axis, exchange(ref, dst, left, axis)))
+            ref, left = dst, left_after(first_axes + then_axes)
+        straight[name] = []
+        if left:
+            first, second = left
+            mine = 2 * bits[first] + bits[second]
+            for offset in range(1, 4):
                 place = (mine + offset) % 4
-                target = me
-                for each, bit in zip(rest, (place // 2, place % 2)):
-                    target = target + STRIDES[each] * (bit - bits[each])
-                view, landing = (place // 2, place % 2), (offset,)
-                if name in CHUNKS:
-                    view += half_of(name, pair)
-                    landing += (slice(None), pl.ds(0, 128 * len(CHUNKS[name][pair])))
-                else:
-                    pair = me_pair
-                far_copies[name].append(
-                    copy(getattr(n, "r2_" + name).at[view], n_far(name).at[landing], (pair, target))
+                target = me + STRIDES[first] * (place // 2 - bits[first])
+                target = target + STRIDES[second] * (place % 2 - bits[second])
+                straight[name].append(
+                    copy(
+                        ref.at[place // 2, place % 2],
+                        getattr(n, "far_" + name).at[offset],
+                        (me_pair, target),
+                    )
                 )
-        if name != DOWN and name not in CHUNKS:
-            pair_copies[name] = copy(getattr(n, "to_" + name), getattr(n, "from_" + name), partner)
+
+    def added(step):
+        src, dst, left, axis, each = step
+        each.wait()
+        for place in places(len(left) - 1):
+            mine = src[index_at(left, axis, bits[axis], place)].astype(F32)
+            at = place or (slice(None),) * 2
+            yield at, mine + dst[at].astype(F32)
 
     def core_start(name):
         if inside:
             core_copies[name].start()
+
+    def hand_over(name, ref, sums):
+        half = getattr(n, "half_" + name)
+        for at, total in sums:
+            total = total.astype(BF16)
+            if name == DOWN:
+                height = total.shape[0] // 2
+                own, others = total[:height], total[height:]
+            else:
+                width = total.shape[1] // 2
+                own, others = total[:, :width], total[:, width:]
+            half[at] = own
+            ref[at + half_of(name, 1)] = others
+        go_on(name)
+        pair_copies[name].start()
+
+    def go_on(name):
+        if after[name]:
+            after[name][0][-1].start()
+        else:
+            for each in straight[name]:
+                each.start()
 
     def core_done(name):
         if not inside:
             return
         core_copies[name].wait()
         g, r1 = getattr(n, "g_" + name), getattr(n, "r1_" + name)
-        for place in places(3):
-            total = (g[place + (core,)].astype(F32) + r1[place].astype(F32)).astype(BF16)
-            if name == DOWN:
-                height = total.shape[0] // 2
-                n.half_down[place] = total[:height]
-                r1[place + half_of(name, 1)] = total[height:]
-            else:
-                r1[place] = total
-        if name == DOWN:
-            pair_copies[name].start()
-        axis_copies[name][0].start()
+        sums = (
+            (place, g[place + (core,)].astype(F32) + r1[place].astype(F32)) for place in places(3)
+        )
+        if not before[name]:
+            hand_over(name, r1, sums)
+            return
+        for at, total in sums:
+            r1[at] = total.astype(BF16)
+        before[name][0][-1].start()
 
     def axis_done(name, i=0):
         if not inside:
             return
-        axis = ROUTES[name][i]
-        left = left_after(name, i)
-        axis_copies[name][i].wait()
-        src = n.half_down if name == DOWN else getattr(n, f"r{i + 1}_{name}")
-        dst = getattr(n, f"r{i + 2}_{name}")
-        for place in places(len(left) - 1):
-            mine = src[index_at(left, axis, bits[axis], place)].astype(F32)
-            at = place or (slice(None),) * 2
-            total = mine + dst[at].astype(F32)
-            if place:
-                dst[at] = total.astype(BF16)
-        if i + 1 < len(ROUTES[name]):
-            axis_copies[name][i + 1].start()
-        elif len(left) == 1:
-            to_pair(name, total)
-        else:
-            for each in far_copies[name]:
-                each.start()
-
-    def to_pair(name, total):
-        width = total.shape[1] // 2
-        getattr(n, "to_" + name)[...] = total[:, width:].astype(BF16)
-        pair_copies[name].start()
-        put(name, total[:, :width])
-
-    def far_total(name, pair):
-        r2, far = getattr(n, "r2_" + name), n_far(name)
-        total = None
-        if pair == 0 or name == DOWN:
-            first, second = left_after(name, 1)
-            view = (bits[first], bits[second])
-            total = r2[view + half_of(name, 0) if name in CHUNKS else view].astype(F32)
-        for k in range(3) if pair == 0 or name == DOWN else range(3, 7):
-            far_copies[name][k].wait_recv()
-            part = far[(k + 1) % 4]
-            if name in CHUNKS:
-                part = part[:, : 128 * len(CHUNKS[name][pair])]
-            part = part.astype(F32)
-            total = part if total is None else total + part
-        return total
+        step = before[name][i]
+        if i + 1 == len(before[name]):
+            hand_over(name, step[1], added(step))
+            return
+        for at, total in added(step):
+            step[1][at] = total.astype(BF16)
+        before[name][i + 1][-1].start()
+
+    def then_done(name):
+        if not inside:
+            return
+        step = after[name][0]
+        for at, total in added(step):
+            if straight[name]:
+                step[1][at] = total.astype(BF16)
+            else:
+                put(name, total)
+        for each in straight[name]:
+            each.start()
 
     def far_done(name):
         if not inside:
             return
-        total = far_total(name, 0)
-        if name in pair_copies and name != DOWN:
-            to_pair(name, total)
-        else:
-            put(name, total)
-
-    def far_done_target(name):
+        ref = after[name][0][1] if after[name] else getattr(n, "half_" + name)
+        first, second = straight_axes(name)
+        total = ref[bits[first], bits[second]].astype(F32)
+        for offset in range(1, 4):
+            straight[name][offset - 1].wait_recv()
+            total += getattr(n, "far_" + name)[offset].astype(F32)
+        put(name, total)
+
+    def straight_axes(name):
+        first_axes, then_axes = ROUTES[name]
+        return left_after(first_axes + then_axes)
+
+    gain_copies = []
+    if inside:
+        gain_copies.append(copy(n.gain_out.at[0], n.gain_in.at[0], sibling))
+        for k in range(15):
+            offset, pair = (k + 1) % 8, 0 if k < 7 else 1
+            gain_copies.append(
+                copy(
+                    n.gain_out.at[1],
+                    n.gain_in.at[1 + offset],
+                    (pair, 2 * ((me // 2 + offset) % 8) + core),
+                )
+            )
+
+    def gain_step():
         if not inside:
             return
-        if name in CHUNKS:
-            total = far_total(name, 1)
-        elif name == DOWN:
-            pair_copies[name].wait_recv()
-            axis_copies[name][0].start()
-            axis_done(name)
-            total = far_total(name, 1)
-        else:
-            pair_copies[name].wait_recv()
-            total = getattr(n, "from_" + name)[...].astype(F32)
-        put(name, total, 1)
-
-    gain_copies = []
-    if inside:
-        gain_copies = [
-            copy(n.gain_out.at[0], n.gain_in.at[0], sibling),
-            copy(n.gain_out.at[1], n.gain_in.at[1], across[ROW]),
-        ]
-        for k in range(7):
-            offset, pair = (k + 1) % 4, 0 if k < 3 else 1
-            gain_copies.append(
-                copy(
-                    n.gain_out.at[2],
-                    n.gain_in.at[2 + offset],
-                    at_quarter((quarter + offset) % 4, pair),
-                )
-            )
-
-    def gain_step(i):
-        if not inside:
-            return
-        gain_copies[i].wait()
-        n.gain_out[i + 1] = n.gain_out[i] + n.gain_in[i]
-        for each in gain_copies[1:2] if i == 0 else gain_copies[2:]:
+        gain_copies[0].wait()
+        n.gain_out[1] = n.gain_out[0] + n.gain_in[0]
+        for each in gain_copies[1:]:
             each.start()
 
     def gain_owner(pair):
         if not inside:
             n.grad_gains[...] = n.gain_out[0]
             return
-        total = n.gain_out[2] if pair == 0 else None
-        for k in range(3) if pair == 0 else range(3, 7):
-            gain_copies[2 + k].wait_recv()
-            part = n.gain_in[2 + (k + 1) % 4]
+        total = n.gain_out[1] if pair == 0 else None
+        for k in range(7) if pair == 0 else range(7, 15):
+            gain_copies[1 + k].wait_recv()
+            part = n.gain_in[1 + (k + 1) % 8]
             total = part if total is None else total + part
         n.grad_gains[...] = total
 
@@ -881,7 +868,7 @@
 
             @pl.when(s == 0)
             def _():
-                axis_done(DOWN)
+                then_done(DOWN)
                 axis_done(HEAD)
                 core_done(OUT)
 
@@ -897,8 +884,6 @@
             @pl.when(s == 3)
             def _():
                 axis_done(OUT)
-                far_done(HEAD)
-                axis_done(UP_A, 1)
 
         n.gain_out[0, 0:1, :] = jnp.sum(n.gain_sums[0], axis=0, keepdims=True)
         n.gain_out[0, 1:2, :] = jnp.sum(n.gain_sums[1], axis=0, keepdims=True)
@@ -919,16 +904,24 @@
         if inside:
             gain_copies[0].start()
             qkv_product(0, QKV_0)
-            axis_done(UP_B, 1)
             qkv_product(256, QKV_1)
             core_done(QKV_0)
             qkv_product(512, QKV_2, QKV_3)
             core_done(QKV_1)
+            axis_done(UP_A, 1)
+            axis_done(UP_B, 1)
             core_done(QKV_2)
             core_done(QKV_3)
-            gain_step(0)
+            gain_step()
+            far_done(HEAD)
             far_done(DOWN)
-            axis_done(UP_A, 2)
+            axis_done(QKV_0)
+            axis_done(QKV_1)
+            axis_done(QKV_2)
+            axis_done(QKV_3)
+            far_done(OUT)
+            then_done(UP_A)
+            then_done(UP_B)
         else:
             for first in range(0, 3 * d, 256):
                 n.g_qkv[..., first : first + 256] = blocks(
@@ -937,23 +930,13 @@
         for s in range(0, seq_count, 2):
             n.state_out[s * L : (s + 2) * L] = without_pad(n.grad_states, s, d // 2)
             n.q_out[s * L : (s + 2) * L] = without_pad(n.q_rows, s, 128)
-        axis_done(QKV_0)
-        if inside:
-            gain_step(1)
-        axis_done(QKV_1)
-        axis_done(QKV_2)
-        axis_done(QKV_3)
-        far_done(OUT)
-        axis_done(UP_B, 2)
         gain_owner(0)
         for name in CHUNKS:
             far_done(name)
         q_copy.wait_send()
         for s in range(seq_count):
             state_copy(s).wait_send()
-        for each in pair_copies.values():
-            each.wait_send()
-        for each in gain_copies[2:] + [each for sent in far_copies.values() for each in sent]:
+        for each in tuple(pair_copies.values()) + tuple(gain_copies[1:]):
             each.wait_send()
 
     @pl.when(jnp.logical_not(online))
@@ -961,25 +944,38 @@
         stat_first(0.0)
         for i in range(4):
             stat_next(i)
-        far_done_target(DOWN)
+        received = (DOWN, HEAD, UP_A, UP_B, OUT) + tuple(CHUNKS)
+
+        def receive(name):
+            if inside:
+                pair_copies[name].wait_recv()
+                go_on(name)
+
+        receive(DOWN)
         q_copy.wait_recv()
         for s in range(0, seq_count, 2):
             n.q_out[s * L : (s + 2) * L] = without_pad(n.q_half, s, 128)
+        then_done(DOWN)
+        for name in received[1:]:
+            receive(name)
+            if name == UP_B:
+                far_done(DOWN)
         for s in range(seq_count):
             state_copy(s).wait_recv()
             if s % 2:
                 n.state_out[(s - 1) * L : (s + 1) * L] = without_pad(n.state_half, s - 1, d // 2)
-        for name in (HEAD, UP_A, UP_B, OUT):
-            far_done_target(name)
-        if inside:
-            gain_owner(1)
+        far_done(HEAD)
+        far_done(OUT)
+        then_done(UP_A)
+        then_done(UP_B)
+        gain_owner(1)
         for name in CHUNKS:
-            far_done_target(name)
+            far_done(name)
         aims_copy.wait_send()
-        if inside:
-            for each in far_copies[DOWN]:
-                each.wait_send()
-
+
+    for sent in straight.values():
+        for each in sent:
+            each.wait_send()
     if inside:
         stat_next(4)
         n.stats[...] = n.stat_out[5]
@@ -1173,8 +1169,8 @@
         turned_ffn=((d, seq_count * LP), BF16),
         state_half=((seq_count, LP, d // 2), BF16),
         gain_sums=((2, 8, d), F32),
-        gain_out=((3, 8, d), F32),
-        gain_in=((6, 8, d), F32),
+        gain_out=((2, 8, d), F32),
+        gain_in=((9, 8, d), F32),
         count_out=((2, 8, 128), F32),
         count_in=((8, 8, 128), F32),
         stat_out=((6, 8, 128), F32),
@@ -1184,23 +1180,21 @@
     if inside:
         for name in TENSORS:
             scratch["their_" + name] = (new_shapes[name], BF16)
-        scratch["half_down"] = ((2, 2, 2) + halves[DOWN], BF16)
-        for name, route in ROUTES.items():
+        for name, (first_axes, then_axes) in ROUTES.items():
             if name in CHUNKS:
-                far = (d // 16, 128 * len(CHUNKS[name][0]))
-                shape = (far[0], 2 * far[1])
-            elif name == DOWN:
-                shape, far = piece[DOWN], halves[DOWN]
+                shape = (d // 16, 2 * (CHUNKS[name][1] - CHUNKS[name][0]))
             else:
-                shape = far = (d // 16, ff // 2) if name in (UP_A, UP_B) else piece[name]
-                scratch["to_" + name] = (shape[0], shape[1] // 2), BF16
-                scratch["from_" + name] = (shape[0], shape[1] // 2), BF16
-            scratch["g_" + name] = ((2, 2, 2, 2) + shape, BF16)
-            scratch["r1_" + name] = ((2, 2, 2) + shape, BF16)
-            for i in range(len(route)):
-                scratch[f"r{i + 2}_{name}"] = ((2,) * (2 - i) + (far if name == DOWN else shape), BF16)
-            if len(route) == 1:
-                scratch["far_" + name] = ((4,) + far, BF16)
+                shape = (d // 16, ff // 2) if name in (UP_A, UP_B) else piece[name]
+            half = halves[DOWN] if name == DOWN else (shape[0], shape[1] // 2)
+            scratch["g_" + name] = (2, 2, 2, 2) + shape, BF16
+            for i in range(len(first_axes) + 1):
+                scratch[f"r{i + 1}_{name}"] = (2,) * (3 - i) + shape, BF16
+            left = 3 - len(first_axes)
+            scratch["half_" + name] = (2,) * left + half, BF16
+            if then_axes:
+                scratch["then_" + name] = (2,) * (left - 1) + half, BF16
+            if left - len(then_axes) == 2:
+                scratch["far_" + name] = (4,) + half, BF16
     names = list(inputs) + list(outputs) + list(scratch) + ["send_sem", "recv_sem", "load_sem"]
     in_vmem = pl.BlockSpec(memory_space=pltpu.VMEM)
     in_smem = pl.BlockSpec(memory_space=pltpu.SMEM)

time: 91.5 us -> 88.5 us (0.967)
  Pallas kernels: 90.5 us -> 87.5 us
    pallas_call x1, Pallas kernels: 87.1 us -> 84.2 us  [local(): pl.pallas_call(functools.partial(layer_kernel, names, data_count, inside)...]
where the time goes in v4:
time: 88.5 us; the launch traced here: 88.4 us
  Pallas kernels  87.5 us (99%)
    pallas_call x1, Pallas kernels, local(): pl.pallas_call(functools.partial(layer_kernel, names, data_count, inside)...  84.2 us
    pallas_call x1, Pallas kernels, local(): pl.pallas_call(functools.partial(finish_kernel, list(moved), list(worked)...  3.38 us

profile of v4, /device:TPU:0, one launch (start us, length us, event | category | flops | bytes accessed | tf_op | source)
XLA Modules:
  0.0 88.4 jit_solution(14512620448002713842)
XLA Ops:
  0.6 84.2 %layer.1 = (bf16[1184,128]{1,0:T(8,128)(2,1)}, bf16[1184,256]{1,0:T(8,128)(2,1)}, f32[8,512]{1,0:T(8,128)}, f32[8,512]{1,0:T(8,128)}, f32[8,128]{1,0:T(8,128)}, ...) custom-call(bf16[1184,512]{1,0:T(8,128)(2,1)} %bitcast.14, ...), custom_call_target="tpu_custom_call" | custom-call | tf_op jit(solution)/shard_map/layer/pallas_call | solution.py:1202
  84.8 3.4 %finish.1 = (bf16[1184,128]{1,0:T(8,128)(2,1)}, bf16[1184,256]{1,0:T(8,128)(2,1)}, f32[1,32]{1,0:T(1,128)}, f32[32,768]{1,0:T(8,128)}, f32[32,256]{1,0:T(8,128)}...) custom-call(bf16[1184,128]{1,0:T(8,128)(2,1)} %get-tuple-element.45., ...), custom_call_target="tpu_custom_call" | custom-call | tf_op jit(solution)/shard_map/finish/pallas_call | solution.py:1232

commit v5 on v4

--- a/solution.py
+++ b/solution.py
@@ -193,9 +193,9 @@
     x = rows(n.x).astype(F32)
     normed = (x * inverse_rms(x) * n.gains[0:1, :]).astype(BF16)
     n.normed_one[both] = split(normed)
-    for first in range(0, 3 * d, 256):
-        n.qkv[both, :, first : first + 256] = split(
-            dot_nn(normed, n.w_qkv[:, first : first + 256])
+    for first in range(0, 3 * d, 512):
+        n.qkv[both, :, first : first + 512] = split(
+            dot_nn(normed, n.w_qkv[:, first : first + 512])
         )
     attend(n, [(s + i, pair) for i in range(2) for pair in range(d // 128)], d)
 
@@ -247,11 +247,11 @@
     both = pl.ds(s, 2)
     ff = n.w_up.shape[1]
     grad_ffn = n.grad_ffn[both].reshape(2 * LP, -1)
-    for first in range(0, ff, 256):
-        grad_active = dot_nt(grad_ffn, n.w_down[first : first + 256, :])
-        slope = n.slope[both, :, first : first + 256].astype(F32)
-        n.slope[both, :, first : first + 256] = (
-            grad_active.reshape(2, LP, 256) * slope
+    for first in range(0, ff, 512):
+        grad_active = dot_nt(grad_ffn, n.w_down[first : first + 512, :])
+        slope = n.slope[both, :, first : first + 512].astype(F32)
+        n.slope[both, :, first : first + 512] = (
+            grad_active.reshape(2, LP, 512) * slope
         ).astype(BF16)
 
 

time: 88.5 us -> 88.5 us (level)
  no operation moved by 1% of the time
where the time goes in v5:
time: 88.5 us; the launch traced here: 88.4 us
  Pallas kernels  87.5 us (99%)
    pallas_call x1, Pallas kernels, local(): pl.pallas_call(functools.partial(layer_kernel, names, data_count, inside)...  84.2 us
    pallas_call x1, Pallas kernels, local(): pl.pallas_call(functools.partial(finish_kernel, list(moved), list(worked)...  3.38 us

profile of v5, /device:TPU:0, one launch (start us, length us, event | category | flops | bytes accessed | tf_op | source)
XLA Modules:
  0.0 88.4 jit_solution(14512620448002713842)
XLA Ops:
  0.6 84.2 %layer.1 = (bf16[1184,128]{1,0:T(8,128)(2,1)}, bf16[1184,256]{1,0:T(8,128)(2,1)}, f32[8,512]{1,0:T(8,128)}, f32[8,512]{1,0:T(8,128)}, f32[8,128]{1,0:T(8,128)}, ...) custom-call(bf16[1184,512]{1,0:T(8,128)(2,1)} %bitcast.14, ...), custom_call_target="tpu_custom_call" | custom-call | tf_op jit(solution)/shard_map/layer/pallas_call | solution.py:1202
  84.8 3.4 %finish.1 = (bf16[1184,128]{1,0:T(8,128)(2,1)}, bf16[1184,256]{1,0:T(8,128)(2,1)}, f32[1,32]{1,0:T(1,128)}, f32[32,768]{1,0:T(8,128)}, f32[32,256]{1,0:T(8,128)}...) custom-call(bf16[1184,128]{1,0:T(8,128)(2,1)} %get-tuple-element.45., ...), custom_call_target="tpu_custom_call" | custom-call | tf_op jit(solution)/shard_map/finish/pallas_call | solution.py:1232
